TPU v7x, 256 devices: a whole 4x4x8 slice. The times are simulated.
256 devices in a mesh: role: 2 (over core), grp: 4 (over x), dev: 32 (over z, y).
Axes of the slice: x: 4, y: 4, z: 8, core: 2. Of those that a mesh axis runs over, the one named last changes fastest.
Arguments:
- pool_pages: bfloat16 [2, 4, 32, 24, 64, 576], P('role', 'grp', 'dev'), may hold values from -8 to 8
- kv_gain: float32 [512], replicated, may hold values from 0.25 to 1.75
- queries: bfloat16 [48, 4, 128, 576], P('grp', None, ('role', 'dev')), may hold values from -64 to 64
- decode_latent: bfloat16 [48, 4, 576], P('grp'), may hold values from -8 to 8
- served_request: int32 [48], replicated, may hold values from 0 to 47, each once
- resident_pages: int32 [4, 12], P('grp'), may hold values from 1 to 384, 768 in all within a row
- resident_tail: int32 [4, 12], P('grp'), may hold values from 1 to 64
- page_dest: int32 [4, 32, 24], P('grp'), may hold values from 0 to 63, as said below
Outputs:
- attention: bfloat16 [48, 4, 128, 512], P('grp', None, ('role', 'dev'))
- received_cache: bfloat16 [4, 32, 64, 64, 576], P('grp', 'dev')
Inputs may be any that keep to these rules, and one draw needn't show every extreme that they name: `page_dest`: within each group and prefill device the values are distinct. At most 2 pages of one prefill device go to one owner; in each group one owner receives exactly 2 pages from every prefill device. `resident_pages`: the counts of each group sum to 768. `served_request`: each request appears once.
All inputs are finite; a program needn't handle non-finite values.
Results may differ from a plain program's by a relative error of at most 0.0015.
The roundings to bfloat16 on the way count: a program that leaves them out, or rounds other values in their place, can miss the bound.
Values may be sent and summed in bfloat16 or wider, within the bound.
A program may use at most 128 MiB of HBM per device.

v0:
```python
import jax
import jax.numpy as jnp
from jax import lax
from jax.sharding import PartitionSpec as P

logit_scale_factor = 192.0 ** (-0.5)
epsilon = 1e-06
lowest = -1e30


def from_partner(value, axis, distance):
    mask = 2**distance
    pairs = [(source, source ^ mask) for source in range(lax.axis_size(axis))]
    return lax.ppermute(value, axis, pairs)


def rotate(rope_part, positions):
    halfway = rope_part.shape[-1] // 2
    frequency = 10000.0 ** (-jnp.arange(halfway, dtype=jnp.float32) / halfway)
    angles = positions[..., None].astype(jnp.float32) * frequency
    leading = rope_part[..., :halfway]
    trailing = rope_part[..., halfway:]
    cosine = jnp.cos(angles)
    sine_part = jnp.sin(angles)
    return jnp.concatenate(
        [leading * cosine - trailing * sine_part, trailing * cosine + leading * sine_part], axis=-1
    )


def finish_keys(source, kv_gain, positions):
    latent_width = kv_gain.shape[0]
    widened = source.astype(jnp.float32)
    latent = widened[..., :latent_width]
    mean_square = jnp.mean(latent * latent, axis=-1, keepdims=True)
    normed = latent * lax.rsqrt(mean_square + epsilon) * kv_gain
    return jnp.concatenate(
        [normed, rotate(widened[..., latent_width:], positions)], axis=-1
    ).astype(jnp.bfloat16)


def largest_block(count, limit):
    return max([trial for trial in range(1, limit + 1) if count % trial == 0])


def attend(pages, requests, valid_len, query_rows, new_keys, adders, block_size, latent_width):
    req_count, row_count, key_width = query_rows.shape
    step_count = new_keys.shape[1]
    heads_here = row_count // step_count
    page_len = pages.shape[1]
    logit_scores = (
        jnp.einsum("rtk,rqk->rtq", new_keys, query_rows, preferred_element_type=jnp.float32)
        * logit_scale_factor
    )
    step_of_row = jnp.arange(row_count) // heads_here
    visible = (jnp.arange(step_count)[:, None] <= step_of_row[None, :])[None] & adders[
        :, None, None
    ]
    logit_scores = jnp.where(visible, logit_scores, lowest)
    running_max = jnp.max(logit_scores, axis=1)
    unnormed = jnp.where(visible, jnp.exp(logit_scores - running_max[:, None, :]), 0.0)
    running_sum = jnp.sum(unnormed, axis=1)
    running_out = jnp.einsum(
        "rtq,rtc->rqc",
        unnormed.astype(jnp.bfloat16),
        new_keys[..., :latent_width],
        preferred_element_type=jnp.float32,
    )
    block_count = pages.shape[0] // block_size
    stacked = (
        pages.reshape(block_count, block_size, page_len, key_width),
        requests.reshape(block_count, block_size),
        valid_len.reshape(block_count, block_size),
    )

    def page_step(state_in, block_data):
        running_out, running_sum, running_max = state_in
        block_of_keys, block_req, block_len = block_data
        local_queries = query_rows[block_req]
        logit_scores = (
            jnp.einsum(
                "zdi,zli->zdl", block_of_keys, local_queries, preferred_element_type=jnp.float32
            )
            * logit_scale_factor
        )
        visible = (jnp.arange(page_len)[None, :] < block_len[:, None])[:, :, None]
        logit_scores = jnp.where(visible, logit_scores, lowest)
        page_max = jnp.max(logit_scores, axis=1)
        unnormed = jnp.where(visible, jnp.exp(logit_scores - page_max[:, None, :]), 0.0)
        page_sum = jnp.sum(unnormed, axis=1)
        page_out = jnp.einsum(
            "btq,btc->bqc",
            unnormed.astype(jnp.bfloat16),
            block_of_keys[..., :latent_width],
            preferred_element_type=jnp.float32,
        )
        member = block_req[None, :] == jnp.arange(req_count)[:, None]
        block_max = jnp.max(jnp.where(member[:, :, None], page_max[None], lowest), axis=1)
        new_max = jnp.maximum(running_max, block_max)
        carry_over = jnp.exp(running_max - new_max)
        factor = jnp.exp(page_max - new_max[block_req])
        running_out = (
            (running_out * carry_over[..., None]).at[block_req].add(page_out * factor[..., None])
        )
        running_sum = (running_sum * carry_over).at[block_req].add(page_sum * factor)
        return ((running_out, running_sum, new_max), None)

    (running_out, running_sum, running_max), _ = lax.scan(
        page_step, (running_out, running_sum, running_max), stacked
    )
    return (running_out, running_sum, running_max)


def per_device(
    pool_pages,
    kv_gain,
    queries,
    decode_latent,
    served_request,
    resident_pages,
    resident_tail,
    page_dest,
):
    owners = lax.axis_size("dev")
    pool_index = lax.axis_index("role")
    group_index = lax.axis_index("grp")
    owner_index = lax.axis_index("dev")
    own_pages = pool_pages[0, 0, 0]
    pages_dev, page_len, key_width = own_pages.shape
    latent_width = kv_gain.shape[0]
    req_grp = resident_pages.shape[1]
    per_prompt = pages_dev // req_grp
    capacity = 2 * max(1, pages_dev // owners)
    counts = resident_pages[0]
    tail_len = resident_tail[0]
    res_len = page_len * (counts - 1) + tail_len
    page_ids = jnp.arange(pages_dev, dtype=jnp.int32)
    prompt_page = page_ids // per_prompt
    positions = (
        res_len[prompt_page][:, None]
        + ((owner_index * per_prompt + page_ids % per_prompt) * page_len)[:, None]
        + jnp.arange(page_len, dtype=jnp.int32)[None, :]
    )
    fresh_keys = finish_keys(own_pages, kv_gain, positions)
    targets = page_dest[0]
    local_target_pages = lax.dynamic_index_in_dim(targets, owner_index, 0, keepdims=False)
    outgoing = (
        jnp.zeros((owners * capacity, page_len, key_width), jnp.bfloat16)
        .at[local_target_pages]
        .set(fresh_keys)
    )
    at_prefill = pool_index == 0
    routed = lax.all_to_all(outgoing, "dev", split_axis=0, concat_axis=0, tiled=True)
    partner_routed, partner_pages = from_partner((routed, own_pages), "role", 0)
    arrived = jnp.where(at_prefill, routed, partner_routed)
    resident = jnp.where(at_prefill, partner_pages, own_pages)
    local_slot = targets - owner_index * capacity
    matches = local_slot[:, None, :] == jnp.arange(capacity)[None, :, None]
    slot_used = jnp.any(matches, axis=2).reshape(-1)
    slot_req = jnp.sum(jnp.where(matches, prompt_page[None, None, :], 0), axis=2).reshape(-1)
    run_ends = jnp.cumsum(counts)
    starts = run_ends - counts
    flat_index = page_ids * owners + owner_index
    res_req = jnp.sum((flat_index[:, None] >= run_ends[None, :]).astype(jnp.int32), axis=1)
    res_page = flat_index - starts[res_req]
    res_valid = jnp.where(res_page < counts[res_req] - 1, page_len, tail_len[res_req])
    all_pages = jnp.concatenate([resident, arrived], axis=0)
    all_req = jnp.concatenate([res_req, slot_req])
    all_valid = jnp.concatenate([res_valid, jnp.where(slot_used, page_len, 0)])
    arrival_q, arrival_latent = (
        lax.all_gather(queries, "grp", axis=0, tiled=True),
        lax.all_gather(decode_latent, "grp", axis=0, tiled=True),
    )
    serving = lax.dynamic_slice_in_dim(served_request, group_index * req_grp, req_grp)
    served_q = arrival_q[serving]
    served_latent = arrival_latent[serving]
    pool_queries = lax.all_gather(served_q, "dev", axis=2, tiled=True)
    step_count = pool_queries.shape[1]
    heads_here = pool_queries.shape[2]
    head_share = heads_here // owners
    query_rows = pool_queries.reshape(req_grp, step_count * heads_here, key_width)
    span_len = per_prompt * page_len * owners
    new_keys = finish_keys(
        served_latent,
        kv_gain,
        res_len[:, None] + span_len + jnp.arange(step_count, dtype=jnp.int32)[None, :],
    )
    adders = jnp.arange(req_grp) % owners == owner_index
    block_size = largest_block(all_pages.shape[0], 24)
    running_out, running_sum, running_max = attend(
        all_pages, all_req, all_valid, query_rows, new_keys, adders, block_size, latent_width
    )
    out_heads = running_out.reshape(req_grp, step_count, heads_here, latent_width)
    sum_heads = running_sum.reshape(req_grp, step_count, heads_here)
    max_heads = running_max.reshape(req_grp, step_count, heads_here)
    out_parts = lax.all_to_all(out_heads, "dev", split_axis=2, concat_axis=0, tiled=True)
    sum_parts = lax.all_to_all(sum_heads, "dev", split_axis=2, concat_axis=0, tiled=True)
    max_parts = lax.all_to_all(max_heads, "dev", split_axis=2, concat_axis=0, tiled=True)
    item_count = out_parts.shape[1]
    out_parts = out_parts.reshape(owners, req_grp, item_count, head_share, latent_width)
    sum_parts = sum_parts.reshape(owners, req_grp, item_count, head_share)
    max_parts = max_parts.reshape(owners, req_grp, item_count, head_share)
    overall = jnp.max(max_parts, axis=0)
    factor = jnp.exp(max_parts - overall)
    numerator = jnp.sum(out_parts * factor[..., None], axis=0)
    denominator = jnp.sum(sum_parts * factor, axis=0)
    attention = (numerator / denominator[..., None]).astype(jnp.bfloat16)
    return (attention, arrived[None, None])


def solution(mesh):
    in_specs = (
        P("role", "grp", "dev", None, None, None),
        P(),
        P("grp", None, ("role", "dev"), None),
        P("grp", None, None),
        P(),
        P("grp", None),
        P("grp", None),
        P("grp", None, None),
    )
    out_specs = (P("grp", None, ("role", "dev"), None), P("grp", "dev", None, None, None))
    return jax.shard_map(
        per_device, mesh=mesh, in_specs=in_specs, out_specs=out_specs, check_vma=False
    )
```

profile of v0, /device:TPU:16, one launch (start us, length us, event | category | flops | bytes accessed | tf_op | source)
XLA Modules:
  0.0 610.1 jit_solution(17791488691733208133)
XLA Ops:
  7.2 0.9 dynamic-slice_reduce_fusion
  8.1 0.8 reduce-window.8
  10.4 2.0 bitcast_convert_fusion
  12.7 3.6 fusion.20
  17.0 3.1 broadcast_in_dim.80
  20.2 5.7 scatter_fusion.1
  25.9 11.8 %all-to-all-start = ((bf16[64,64,576]{2,1,0:T(8,128)(2,1)}), bf16[64,64,576]{2,1,0:T(8,128)(2,1)}, u32[]{:S(2)}, u32[]{:S(2)}) async-start(bf16[64,64,576]{2,1,0:T(8,128)(2,1)} %scatter_fusion.1), calls=%async_computation | async-start | bytes 10485760 | tf_op jit(solution)/shard_map/all_to_all | solution.py:152
  37.9 13.0 %all_gather.10 = bf16[48,4,2,576]{3,1,2,0:T(4,128)(2,1)S(1)} all-gather(bf16[12,4,2,576]{3,1,2,0:T(4,128)(2,1)S(1)} %copy.58), channel_id=1, replica_groups=mesh['role'=2,'grp'=4,'dev'=32] {'grp'}, dimensions={0}, use_global_device_ids=true | all-gather | bytes 552960 | tf_op jit(solution)/shard_map/all_gather | solution.py:170
  52.3 125.1 %all-to-all-done = bf16[64,64,576]{2,1,0:T(8,128)(2,1)} async-done(((bf16[64,64,576]{2,1,0:T(8,128)(2,1)}), bf16[64,64,576]{2,1,0:T(8,128)(2,1)}, u32[]{:S(2)}, u32[]{:S(2)}) %all-to-all-start) | async-done | bytes 4718624 | tf_op jit(solution)/shard_map/all_to_all | solution.py:152
  181.0 12.7 %all_gather.9 = bf16[48,4,576]{2,1,0:T(4,128)(2,1)S(1)} all-gather(bf16[12,4,576]{2,1,0:T(4,128)(2,1)S(1)} %copy-done.6), channel_id=1, replica_groups=mesh['role'=2,'grp'=4,'dev'=32] {'grp'}, dimensions={0}, use_global_device_ids=true | all-gather | bytes 276480 | tf_op jit(solution)/shard_map/all_gather | solution.py:171
  194.9 2.4 broadcast_select_fusion.1
  197.3 3.1 copy.60
  200.4 1.1 fusion.56
  201.7 3.8 fusion.34
  205.5 3.0 broadcast_select_fusion
  208.6 4.4 pad_maximum_fusion
  213.1 206.8 %while.14 = (s32[]{:T(128)}, f32[12,256,512]{2,1,0:T(8,128)}, f32[12,256]{1,0:T(8,128)S(1)}, f32[12,256]{1,0:T(8,128)S(1)}, s32[4,22]{1,0:T(4,128)S(1)}, /*index...) while((s32[]{:T(128)}, f32[12,256,512]{2,1,0:T(8,128)}, ...), condition=%wide.region_15.16_spmd, body=%wide.region_9.15_spmd.sunk | while | flops 795068608 | bytes 89242400 | solution.py:107
  213.2 1.7 dynamic-slice_bitcast_fusion.2
  214.9 7.3 %gather_fusion = bf16[22,256,576]{2,1,0:T(8,128)(2,1)} fusion(bf16[12,256,576]{2,1,0:T(8,128)(2,1)} %get-tuple-element.183, s32[1024]{0:T(1024)S(1)} %pad_clamp_fusion.5), kind=kCustom, calls=%fused_computation.clone.1 | custom fusion | bytes 12976216 | tf_op jit(solution)/shard_map/while/body/eval_jaxpr/gather | solution.py:78
  222.2 4.4 fusion.78
  228.5 5.8 broadcast_multiply_fusion.4
  234.3 5.9 broadcast_multiply_fusion.5
  240.2 24.7 %scatter_fusion = f32[12,256,512]{2,1,0:T(8,128)} fusion(f32[12,256,512]{2,1,0:T(8,128)} %broadcast_multiply_fusion.4, s32[22]{0:T(128)S(1)} %fusion.76, f32[22,256,512]{2,1,0:T(8,128)} %broadcast_multiply_fusion.5), kind=kCustom, calls=%fused_computation.8.clone.1 | custom fusion | flops 2883584 | bytes 34603096 | tf_op jit(solution)/shard_map/while/body/eval_jaxpr/scatter-add | solution.py:102
  264.9 1.7 dynamic-slice_bitcast_fusion.2
  266.6 7.2 %gather_fusion = bf16[22,256,576]{2,1,0:T(8,128)(2,1)} fusion(bf16[12,256,576]{2,1,0:T(8,128)(2,1)} %get-tuple-element.183, s32[1024]{0:T(1024)S(1)} %pad_clamp_fusion.5), kind=kCustom, calls=%fused_computation.clone.1 | custom fusion | bytes 12976216 | tf_op jit(solution)/shard_map/while/body/eval_jaxpr/gather | solution.py:78
  273.8 4.4 fusion.78
  280.1 5.8 broadcast_multiply_fusion.4
  285.9 5.9 broadcast_multiply_fusion.5
  291.8 24.5 %scatter_fusion = f32[12,256,512]{2,1,0:T(8,128)} fusion(f32[12,256,512]{2,1,0:T(8,128)} %broadcast_multiply_fusion.4, s32[22]{0:T(128)S(1)} %fusion.76, f32[22,256,512]{2,1,0:T(8,128)} %broadcast_multiply_fusion.5), kind=kCustom, calls=%fused_computation.8.clone.1 | custom fusion | flops 2883584 | bytes 34603096 | tf_op jit(solution)/shard_map/while/body/eval_jaxpr/scatter-add | solution.py:102
  316.4 1.7 dynamic-slice_bitcast_fusion.2
  318.0 7.2 %gather_fusion = bf16[22,256,576]{2,1,0:T(8,128)(2,1)} fusion(bf16[12,256,576]{2,1,0:T(8,128)(2,1)} %get-tuple-element.183, s32[1024]{0:T(1024)S(1)} %pad_clamp_fusion.5), kind=kCustom, calls=%fused_computation.clone.1 | custom fusion | bytes 12976216 | tf_op jit(solution)/shard_map/while/body/eval_jaxpr/gather | solution.py:78
  325.2 4.4 fusion.78
  331.5 5.8 broadcast_multiply_fusion.4
  337.4 5.8 broadcast_multiply_fusion.5
  343.2 24.5 %scatter_fusion = f32[12,256,512]{2,1,0:T(8,128)} fusion(f32[12,256,512]{2,1,0:T(8,128)} %broadcast_multiply_fusion.4, s32[22]{0:T(128)S(1)} %fusion.76, f32[22,256,512]{2,1,0:T(8,128)} %broadcast_multiply_fusion.5), kind=kCustom, calls=%fused_computation.8.clone.1 | custom fusion | flops 2883584 | bytes 34603096 | tf_op jit(solution)/shard_map/while/body/eval_jaxpr/scatter-add | solution.py:102
  367.8 1.7 dynamic-slice_bitcast_fusion.2
  369.5 7.2 %gather_fusion = bf16[22,256,576]{2,1,0:T(8,128)(2,1)} fusion(bf16[12,256,576]{2,1,0:T(8,128)(2,1)} %get-tuple-element.183, s32[1024]{0:T(1024)S(1)} %pad_clamp_fusion.5), kind=kCustom, calls=%fused_computation.clone.1 | custom fusion | bytes 12976216 | tf_op jit(solution)/shard_map/while/body/eval_jaxpr/gather | solution.py:78
  376.7 4.4 fusion.78
  383.0 5.8 broadcast_multiply_fusion.4
  388.9 5.9 broadcast_multiply_fusion.5
  394.7 25.1 %scatter_fusion = f32[12,256,512]{2,1,0:T(8,128)} fusion(f32[12,256,512]{2,1,0:T(8,128)} %broadcast_multiply_fusion.4, s32[22]{0:T(128)S(1)} %fusion.76, f32[22,256,512]{2,1,0:T(8,128)} %broadcast_multiply_fusion.5), kind=kCustom, calls=%fused_computation.8.clone.1 | custom fusion | flops 2883584 | bytes 34603096 | tf_op jit(solution)/shard_map/while/body/eval_jaxpr/scatter-add | solution.py:102
  420.7 7.9 %all-to-all-start.3 = ((f32[12,4,64]{0,1,2:T(4,128)}), f32[12,4,64]{0,1,2:T(4,128)S(1)}, u32[]{:S(2)}, u32[]{:S(2)}) async-start(f32[12,4,64]{0,1,2:T(4,128)} %copy.68), calls=%async_computation.3 | async-start | bytes 262144 | tf_op jit(solution)/shard_map/all_to_all | solution.py:196
  429.4 7.6 %all-to-all-done.3 = f32[12,4,64]{0,1,2:T(4,128)S(1)} async-done(((f32[12,4,64]{0,1,2:T(4,128)}), f32[12,4,64]{0,1,2:T(4,128)S(1)}, u32[]{:S(2)}, u32[]{:S(2)}) %all-to-all-start.3) | async-done | bytes 12320 | tf_op jit(solution)/shard_map/all_to_all | solution.py:196
  437.0 5.8 all-to-all-start.2
  442.8 9.5 %copy.64 = f32[12,4,64,512]{3,1,0,2:T(4,128)} copy(f32[12,4,64,512]{3,2,1,0:T(8,128)} %bitcast.65) | data formatting | bytes 12582912 | tf_op jit(solution)/shard_map/reshape | solution.py:192
  452.3 9.9 %all-to-all-start.1 = ((f32[12,4,64,512]{3,1,0,2:T(4,128)}), f32[12,4,64,512]{3,1,0,2:T(4,128)}, u32[]{:S(2)}, u32[]{:S(2)}) async-start(f32[12,4,64,512]{3,1,0,2:T(4,128)} %copy.64), calls=%async_computation.1 | async-start | bytes 12582912 | tf_op jit(solution)/shard_map/all_to_all | solution.py:195
  463.1 135.1 %all-to-all-done.1 = f32[12,4,64,512]{3,1,0,2:T(4,128)} async-done(((f32[12,4,64,512]{3,1,0,2:T(4,128)}), f32[12,4,64,512]{3,1,0,2:T(4,128)}, u32[]{:S(2)}, u32[]{:S(2)}) %all-to-all-start.1) | async-done | bytes 6291488 | tf_op jit(solution)/shard_map/all_to_all | solution.py:195
  598.2 4.3 multiply_reduce_fusion
  (133 shorter events, 20.3 us)
Async XLA Ops:
  12.4 3.9 copy-start.8
  25.8 11.9 %copy-start.5 = (bf16[12,4,2,576]{3,2,1,0:T(2,128)(2,1)S(1)}, bf16[12,4,2,576]{3,2,1,0:T(2,128)(2,1)}, u32[]{:S(2)}) copy-start(bf16[12,4,2,576]{3,2,1,0:T(2,128)(2,1)} %param.12) | copy-start | bytes 331780
  25.8 11.9 %copy-start.9 = (s32[48]{0:T(128)S(1)}, s32[48]{0:T(128)}, u32[]{:S(2)}) copy-start(s32[48]{0:T(128)} %param.14) | copy-start | bytes 580
  25.8 151.6 %copy-start.4 = (bf16[1,1,1,24,64,576]{5,4,3,2,1,0:T(8,128)(2,1)S(1)}, bf16[1,1,1,24,64,576]{5,4,3,2,1,0:T(8,128)(2,1)}, u32[]{:S(2)}) copy-start(bf16[1,1,1,24,64,576]{5,4,3,2,1,0:T(8,128)(2,1)} %param.10) | copy-start | bytes 5308420
  25.8 152.9 %copy-start = (s32[1,12]{1,0:T(1,128)S(1)}, s32[1,12]{1,0:T(1,128)}, u32[]{:S(2)}) copy-start(s32[1,12]{1,0:T(1,128)} %param.16) | copy-start | bytes 148
  25.8 153.6 %copy-start.1 = (s32[1,12]{1,0:T(1,128)S(1)}, s32[1,12]{1,0:T(1,128)}, u32[]{:S(2)}) copy-start(s32[1,12]{1,0:T(1,128)} %param.15) | copy-start | bytes 148
  25.9 154.3 %copy-start.7 = (s32[1,32,24]{1,2,0:T(8,128)S(1)}, s32[1,32,24]{1,2,0:T(8,128)}, u32[]{:S(2)}) copy-start(s32[1,32,24]{1,2,0:T(8,128)} %param.17) | copy-start | bytes 9220
  25.9 155.1 %copy-start.6 = (bf16[12,4,576]{2,1,0:T(4,128)(2,1)S(1)}, bf16[12,4,576]{2,1,0:T(4,128)(2,1)}, u32[]{:S(2)}) copy-start(bf16[12,4,576]{2,1,0:T(4,128)(2,1)} %param.13) | copy-start | bytes 165892
  25.9 151.5 %all-to-all-start = ((bf16[64,64,576]{2,1,0:T(8,128)(2,1)}), bf16[64,64,576]{2,1,0:T(8,128)(2,1)}, u32[]{:S(2)}, u32[]{:S(2)}) async-start(bf16[64,64,576]{2,1,0:T(8,128)(2,1)} %scatter_fusion.1), calls=%async_computation | async-start | bytes 10485760 | tf_op jit(solution)/shard_map/all_to_all | solution.py:152
  37.7 159.7 %all-gather.3.cloned.1.call-start = ((), (), s32[]{:S(2)}) async-start(), calls=%async_computation.4 | async-start | bytes 4055040 | tf_op jit(solution)/shard_map/all_gather | solution.py:176
  177.4 28.1 %collective-permute-start.1 = (bf16[64,64,576]{2,1,0:T(8,128)(2,1)}, bf16[64,64,576]{2,1,0:T(8,128)(2,1)}, u32[]{:S(2)}, u32[]{:S(2)}) collective-permute-start(bf16[64,64,576]{2,1,0:T(8,128)(2,1)} %all-to-all-done), channel_id=1, source_target_pairs={{0,128},{128,0},{1,129},{129,1},{2,130},{130,2},{3,131},{131,3},{4... | collective-permute-start | bytes 14155784 | tf_op jit(solution)/shard_map/ppermute | solution.py:14
  177.4 17.5 %collective-permute-start = (bf16[24,64,576]{2,1,0:T(8,128)(2,1)S(1)}, bf16[24,64,576]{2,1,0:T(8,128)(2,1)}, u32[]{:S(2)}, u32[]{:S(2)}) collective-permute-start(bf16[24,64,576]{2,1,0:T(8,128)(2,1)S(1)} %bitcast.73), channel_id=1, source_target_pairs={{0,128},{128,0},{1,129},{129,1},{2,130},{130,2},{3,131},{131,3},{4... | collective-permute-start | bytes 5308424 | tf_op jit(solution)/shard_map/ppermute | solution.py:14
  200.4 5.1 copy-start.2
  208.6 4.5 copy-start.3
  420.7 16.3 %all-to-all-start.3 = ((f32[12,4,64]{0,1,2:T(4,128)}), f32[12,4,64]{0,1,2:T(4,128)S(1)}, u32[]{:S(2)}, u32[]{:S(2)}) async-start(f32[12,4,64]{0,1,2:T(4,128)} %copy.68), calls=%async_computation.3 | async-start | bytes 262144 | tf_op jit(solution)/shard_map/all_to_all | solution.py:196
  437.0 15.3 %all-to-all-start.2 = ((f32[12,4,64]{0,1,2:T(4,128)}), f32[12,4,64]{0,1,2:T(4,128)S(1)}, u32[]{:S(2)}, u32[]{:S(2)}) async-start(f32[12,4,64]{0,1,2:T(4,128)} %copy.65), calls=%async_computation.2 | async-start | bytes 262144 | tf_op jit(solution)/shard_map/all_to_all | solution.py:197
  452.3 145.8 %all-to-all-start.1 = ((f32[12,4,64,512]{3,1,0,2:T(4,128)}), f32[12,4,64,512]{3,1,0,2:T(4,128)}, u32[]{:S(2)}, u32[]{:S(2)}) async-start(f32[12,4,64,512]{3,1,0,2:T(4,128)} %copy.64), calls=%async_computation.1 | async-start | bytes 12582912 | tf_op jit(solution)/shard_map/all_to_all | solution.py:195
Sparse Core Ops, SparseCore 0:
  52.4 123.0 all-gather.2
where the time goes:
time: 613 us; the launch traced here: 610 us
  waiting for transfers between devices  268 us (44%)
  other arithmetic  151 us (25%)
  local copies, waits for them, and re-layouts  68.8 us (11%)
  matrix products  46 us (8%)
  starting transfers between devices  36 us (6%)
  blocking collectives  25.7 us (4%)
  between operations  14.4 us (2%)
    all_to_all x1, waiting for transfers between devices, per_device(): lax.all_to_all(out_heads, 'dev', split_axis=2, concat_axis=0, tiled=True)  135 us
    all_to_all x1, waiting for transfers between devices, per_device(): lax.all_to_all(outgoing, 'dev', split_axis=0, concat_axis=0, tiled=True)  125 us
    scatter-add x4, other arithmetic, page_step(): (running_out * carry_over[..., None]).at[block_req]  98.7 us
    gather x4, local copies, waits for them, and re-layouts, page_step(): local_queries = query_rows[block_req]  28.9 us
    dot_general x4, matrix products, page_step(): jnp.einsum('btq,btc->bqc', unnormed.astype(jnp.bfloat16), block_of_keys[....  23.4 us
    mul x4, other arithmetic, page_step(): running_out * carry_over[..., None]  23.4 us
    dot_general x4, matrix products, page_step(): jnp.einsum('zdi,zli->zdl', block_of_keys, local_queries, preferred_elemen...  17.6 us
    all_gather x1, blocking collectives, per_device(): lax.all_gather(queries, 'grp', axis=0, tiled=True)  13 us
  transfers between devices with their start and end apart: 7, of which 3 were waited for; matrix products, arithmetic and copies ran while one was open for 4% of the time, Pallas kernels for 0%

commit v1 on v0

v1 whole, which is shorter than its diff:
```python
import functools

import jax
import jax.numpy as jnp
from jax import lax
from jax.experimental import pallas as pl
from jax.experimental.pallas import tpu as pltpu
from jax.sharding import PartitionSpec as P

logit_scale_factor = 192.0 ** (-0.5)
epsilon = 1e-06
lowest = -1e30

VMEM_LIMIT = 48 * 1024 * 1024
LAT = 512
KDIM = 576
PAGE = 64
OWNERS = 32
RING_Y = 4
RING_Z = 8


def rotate(rope_part, positions):
    halfway = rope_part.shape[-1] // 2
    frequency = 10000.0 ** (-jnp.arange(halfway, dtype=jnp.float32) / halfway)
    angles = positions[..., None].astype(jnp.float32) * frequency
    leading = rope_part[..., :halfway]
    trailing = rope_part[..., halfway:]
    cosine = jnp.cos(angles)
    sine_part = jnp.sin(angles)
    return jnp.concatenate(
        [leading * cosine - trailing * sine_part, trailing * cosine + leading * sine_part], axis=-1
    )


def finish_keys(source, kv_gain, positions):
    widened = source.astype(jnp.float32)
    latent = widened[..., :LAT]
    mean_square = jnp.mean(latent * latent, axis=-1, keepdims=True)
    normed = latent * lax.rsqrt(mean_square + epsilon) * kv_gain
    return jnp.concatenate([normed, rotate(widened[..., LAT:], positions)], axis=-1).astype(
        jnp.bfloat16
    )


def rope_table(positions):
    frequency = 10000.0 ** (-jnp.arange(32, dtype=jnp.float32) / 32)
    angles = positions[..., None].astype(jnp.float32) * frequency
    cosine = jnp.cos(angles)
    sine_part = jnp.sin(angles)
    return jnp.concatenate([cosine, cosine, -sine_part, sine_part], axis=-1)


def finish_kernel(
    inverse_ref, role_ref, own_ref, partner_ref, gain_ref, table_ref, fresh_ref, resident_ref, out_ref
):
    at_prefill = role_ref[0] == 0
    gain = gain_ref[...]

    def one_page(i, _):
        mine = own_ref[i]
        other = partner_ref[i]
        raw = jnp.where(at_prefill, mine, other).astype(jnp.float32)
        resident_ref[i] = jnp.where(at_prefill, other, mine)
        latent = raw[:, :LAT]
        mean_square = jnp.sum(latent * latent, axis=-1, keepdims=True) * (1.0 / LAT)
        normed = latent * lax.rsqrt(mean_square + epsilon) * gain
        rope = raw[:, LAT:]
        swapped = jnp.concatenate([rope[:, 32:], rope[:, :32]], axis=-1)
        table = table_ref[i]
        turned = rope * table[:, :64] + swapped * table[:, 64:]
        fresh_ref[i] = jnp.concatenate([normed, turned], axis=-1).astype(jnp.bfloat16)
        return 0

    lax.fori_loop(0, own_ref.shape[0], one_page, 0)

    def one_slot(t, _):
        page = inverse_ref[t]
        found = fresh_ref[jnp.maximum(page, 0)]
        out_ref[t] = jnp.where(page >= 0, found, jnp.zeros_like(found))
        return 0

    lax.fori_loop(0, OWNERS, one_slot, 0)


def finish_and_pack(inverse, role, own, partner, gain, table):
    pages = own.shape[0]
    smem = pl.BlockSpec(memory_space=pltpu.SMEM)
    vmem = pl.BlockSpec(memory_space=pltpu.VMEM)
    page = jax.ShapeDtypeStruct((pages, PAGE, KDIM), jnp.bfloat16)
    return pl.pallas_call(
        finish_kernel,
        out_shape=(page, page, jax.ShapeDtypeStruct((OWNERS, PAGE, KDIM), jnp.bfloat16)),
        in_specs=[smem, smem, vmem, vmem, vmem, vmem],
        out_specs=(vmem, vmem, vmem),
        compiler_params=pltpu.CompilerParams(vmem_limit_bytes=VMEM_LIMIT),
        cost_estimate=pl.CostEstimate(flops=20_000_000, bytes_accessed=10_000_000, transcendentals=0),
        name="finish_and_pack",
    )(inverse, role, own, partner, gain.reshape(1, LAT), table)


def attend_kernel(
    begin_ref, end_ref, valid_ref, owner_ref,
    q_ref, fresh_ref, resident_ref, newk_ref,
    o_ref, ml_ref,
    acc, m_ref, l_ref,
):
    pair = pl.program_id(0)
    rows = acc.shape[0]

    @pl.when(pair == 0)
    def _():
        ml_ref[...] = jnp.zeros(ml_ref.shape, jnp.float32)

    lane = lax.broadcasted_iota(jnp.int32, (rows, 2 * PAGE), 1)
    low = lane < PAGE
    step_of_row = (lax.broadcasted_iota(jnp.int32, (rows, 2 * PAGE), 0) % 8) // 2

    def weigh(q, keys, visible, m_before):
        s = lax.dot_general(q, keys, (((1,), (1,)), ((), ())), preferred_element_type=jnp.float32)
        s = s * logit_scale_factor
        if visible is not None:
            s = jnp.where(visible, s, lowest)
        m1 = jnp.max(jnp.where(low, s, lowest), axis=1, keepdims=True)
        m2 = jnp.max(jnp.where(low, lowest, s), axis=1, keepdims=True)
        mb = jnp.where(low, m1, m2)
        e = jnp.exp(s - mb)
        if visible is not None:
            e = jnp.where(visible, e, 0.0)
        m_now = jnp.maximum(m1, m2)
        if m_before is not None:
            m_now = jnp.maximum(m_now, m_before)
        f = jnp.where(low, jnp.exp(m1 - m_now), jnp.exp(m2 - m_now))
        l = jnp.sum(e * f, axis=1, keepdims=True)
        wide = e.astype(jnp.bfloat16).astype(jnp.float32) * f
        hi = wide.astype(jnp.bfloat16)
        lo = (wide - hi.astype(jnp.float32)).astype(jnp.bfloat16)
        values = keys[:, :LAT]
        o = jnp.dot(
            jnp.concatenate([hi, lo], axis=1),
            jnp.concatenate([values, values], axis=0),
            preferred_element_type=jnp.float32,
        )
        return m_now, l, o

    def update(q, keys, visible):
        before = m_ref[...]
        m_now, l, o = weigh(q, keys, visible, before)
        carry = jnp.exp(before - m_now)
        m_ref[...] = m_now
        l_ref[...] = l_ref[...] * carry + l
        acc[...] = acc[...] * carry + o

    for jj in range(2):
        j = pair * 2 + jj
        blocks = [
            q_ref[z * RING_Y + y].astype(jnp.float32)[jj * 8 : jj * 8 + 8]
            for y in range(RING_Y)
            for z in range(RING_Z)
        ]
        q = jnp.concatenate(blocks, axis=0).astype(jnp.bfloat16)
        keys = fresh_ref[2 * jj : 2 * jj + 2].reshape(2 * PAGE, KDIM)
        m_now, l, o = weigh(q, keys, None, None)
        m_ref[...] = m_now
        l_ref[...] = l
        acc[...] = o
        begin = begin_ref[j]
        end = end_ref[j]

        def two_pages(i, _):
            first = begin + 2 * i
            second = jnp.minimum(first + 1, end - 1)
            keys = jnp.concatenate([resident_ref[first], resident_ref[second]], axis=0)
            live_first = valid_ref[first]
            live_second = jnp.where(first + 1 < end, valid_ref[second], 0)
            visible = lane < jnp.where(low, live_first, PAGE + live_second)
            update(q, keys, visible)
            return 0

        lax.fori_loop(0, (end - begin + 1) // 2, two_pages, 0)

        @pl.when(j == owner_ref[0])
        def _():
            visible = lane <= jnp.where(lane < 4, step_of_row, -1)
            update(q, newk_ref[...], visible)

        codes, scale = encode(acc[...])
        o_ref[:, jj] = codes.reshape(RING_Y, rows // RING_Y, LAT)
        stats = jnp.where(lane == 16 + j, l_ref[...], jnp.where(lane == 32 + j, scale, ml_ref[...]))
        ml_ref[...] = jnp.where(lane == j, m_ref[...], stats)


def attend(begin, end, valid, owner, q_all, fresh, resident, newk):
    rows = 8 * OWNERS
    smem = pl.BlockSpec(memory_space=pltpu.SMEM)
    pairs = 6
    return pl.pallas_call(
        attend_kernel,
        grid=(pairs,),
        out_shape=(
            jax.ShapeDtypeStruct((RING_Y, 2 * pairs, rows // RING_Y, LAT), jnp.int16),
            jax.ShapeDtypeStruct((rows, 128), jnp.float32),
        ),
        in_specs=[
            smem, smem, smem, smem,
            pl.BlockSpec((OWNERS, 16, KDIM), lambda p: (0, p, 0)),
            pl.BlockSpec((4, PAGE, KDIM), lambda p: (p, 0, 0)),
            pl.BlockSpec((24, PAGE, KDIM), lambda p: (0, 0, 0)),
            pl.BlockSpec((2 * PAGE, KDIM), lambda p: (0, 0)),
        ],
        out_specs=(
            pl.BlockSpec((RING_Y, 2, rows // RING_Y, LAT), lambda p: (0, p, 0, 0)),
            pl.BlockSpec((rows, 128), lambda p: (0, 0)),
        ),
        scratch_shapes=[
            pltpu.VMEM((rows, LAT), jnp.float32),
            pltpu.VMEM((rows, 1), jnp.float32),
            pltpu.VMEM((rows, 1), jnp.float32),
        ],
        compiler_params=pltpu.CompilerParams(vmem_limit_bytes=VMEM_LIMIT),
        cost_estimate=pl.CostEstimate(
            flops=2_000_000_000, bytes_accessed=11_000_000, transcendentals=2_000_000
        ),
        name="attend_pages",
    )(begin, end, valid, owner, q_all, fresh, resident, newk)


MESH_IDS = pl.DeviceIdType.MESH
CODE_TOP = 32767.0
CHUNKS = 2
HALF = 6 // CHUNKS


def greet(devices):
    barrier = pltpu.get_barrier_semaphore()
    for device in devices:
        pl.semaphore_signal(barrier, inc=1, device_id=device, device_id_type=MESH_IDS)
    pl.semaphore_wait(barrier, len(devices))


def merge_stats(blocks):
    lane = lax.broadcasted_iota(jnp.int32, blocks[0].shape, 1)
    top = functools.reduce(jnp.maximum, blocks)
    total = jnp.zeros_like(top)
    weights = []
    for block in blocks:
        part = jnp.exp(jnp.where(lane < 16, block - top, 0.0))
        total = total + part * pltpu.roll(block, 112, 1)
        weights.append(part * pltpu.roll(block, 96, 1))
    return top, total, weights


def column(block, index):
    lane = lax.broadcasted_iota(jnp.int32, block.shape, 1)
    return jnp.sum(jnp.where(lane == index, block, 0.0), axis=1, keepdims=True)


def encode(values):
    scale = jnp.max(jnp.abs(values), axis=1, keepdims=True)
    codes = jnp.floor(values * (CODE_TOP / jnp.maximum(scale, 1e-30)) + 0.5)
    return codes.astype(jnp.int32).astype(jnp.int16), scale * (1.0 / CODE_TOP)


def decode(codes):
    return codes.astype(jnp.int32).astype(jnp.float32)


def join_stats(top, total, scales):
    lane = lax.broadcasted_iota(jnp.int32, top.shape, 1)
    return jnp.where(lane < 16, top, jnp.where(lane < 32, pltpu.roll(total, 16, 1), scales))


def merge_kernel(
    o_ref, ml_ref, out_ref,
    relay_in, direct_in, merged, merged_in, stat_in, mstat, mstat_in,
    zcodes, zin, zstat, zstat_in, values,
    send_y, recv_y, send_z, recv_z,
):
    role = lax.axis_index("role")
    group = lax.axis_index("grp")
    me = lax.axis_index("dev")
    z = me // RING_Y
    y = me % RING_Y

    def at(zz, yy):
        return (role, group, zz * RING_Y + yy)

    up = (y + 1) % RING_Y
    down = (y + 3) % RING_Y
    far = (y + 2) % RING_Y
    greet([at(z, up), at(z, down)] + [at((z + k) % RING_Z, y) for k in range(1, RING_Z)])
    copies = []

    def push(src, dst, sends, recvs, index, target):
        copy = pltpu.make_async_remote_copy(
            src_ref=src, dst_ref=dst, send_sem=sends.at[index], recv_sem=recvs.at[index],
            device_id=target, device_id_type=MESH_IDS,
        )
        copy.start()
        copies.append(copy)
        return copy

    ways = ((up, down), (down, up))
    stat_far, stat_near, relayed, direct = {}, {}, {}, {}
    for way, (ahead, _) in enumerate(ways):
        stat_far[way] = push(ml_ref.at[far], stat_in.at[2 * way], send_y, recv_y, 2 * way, at(z, ahead))
        stat_near[way] = push(
            ml_ref.at[ahead], stat_in.at[2 * way + 1], send_y, recv_y, 2 * way + 1, at(z, ahead)
        )
    for c in range(CHUNKS):
        for way, (ahead, _) in enumerate(ways):
            base = 6 * way + HALF * c
            relayed[c, way] = push(
                o_ref.at[far, pl.ds(base, HALF)], relay_in.at[way, c], send_y, recv_y,
                4 + 2 * c + way, at(z, ahead),
            )
        for way, (ahead, _) in enumerate(ways):
            base = 6 * (1 - way) + HALF * c
            direct[c, way] = push(
                o_ref.at[ahead, pl.ds(base, HALF)], direct_in.at[way, c], send_y, recv_y,
                4 + 2 * CHUNKS + 2 * c + way, at(z, ahead),
            )

    passed, passed_stat = {}, {}
    for c in range(CHUNKS):
        for way, (ahead, _) in enumerate(ways):
            if c == 0:
                stat_far[way].wait_recv()
            relayed[c, way].wait_recv()
            top, total, weights = merge_stats([stat_in[2 * way], ml_ref[ahead]])
            base = 6 * way + HALF * c

            def relay_one(i, scales, way=way, c=c, base=base, ahead=ahead, weights=weights):
                mixed = decode(relay_in[way, c, i]) * column(weights[0], base + i)
                mixed = mixed + decode(o_ref[ahead, base + i]) * column(weights[1], base + i)
                codes, scale = encode(mixed)
                merged[way, c, i] = codes
                lane = lax.broadcasted_iota(jnp.int32, scales.shape, 1)
                return jnp.where(lane == 32 + base + i, scale, scales)

            scales = lax.fori_loop(0, HALF, relay_one, jnp.zeros_like(top))
            mstat[way, c] = join_stats(top, total, scales)
            first = 4 + 4 * CHUNKS + 4 * c + 2 * way
            passed[c, way] = push(
                merged.at[way, c], merged_in.at[way, c], send_y, recv_y, first, at(z, ahead)
            )
            passed_stat[c, way] = push(
                mstat.at[way, c], mstat_in.at[way, c], send_y, recv_y, first + 1, at(z, ahead)
            )

    arrivals = {}
    for c in range(CHUNKS):
        if c == 0:
            for way in range(2):
                stat_near[way].wait_recv()
        stats = []
        for way in range(2):
            passed_stat[c, way].wait_recv()
            passed[c, way].wait_recv()
            direct[c, 1 - way].wait_recv()
            stats.append(merge_stats([ml_ref[y], mstat_in[way, c], stat_in[2 * (1 - way) + 1]]))
        lane = lax.broadcasted_iota(jnp.int32, ml_ref[y].shape, 1)
        scales = jnp.zeros(ml_ref[y].shape, jnp.float32)
        for way in range(2):
            base = 6 * way + HALF * c
            top, total, weights = stats[way]

            def land_one(i, scales, way=way, c=c, base=base, weights=weights):
                mixed = decode(o_ref[y, base + i]) * column(weights[0], base + i)
                mixed = mixed + decode(merged_in[way, c, i]) * column(weights[1], base + i)
                mixed = mixed + decode(direct_in[1 - way, c, i]) * column(weights[2], base + i)
                scale = jnp.maximum(jnp.max(jnp.abs(mixed), axis=1, keepdims=True), 1e-30)
                values[way * HALF + i] = jnp.floor(mixed * (CODE_TOP / scale) + 0.5)
                return jnp.where(lane == 32 + base + i, scale * (1.0 / CODE_TOP), scales)

            scales = lax.fori_loop(0, HALF, land_one, scales)
        use_up = (lane % 16) < 6
        top = jnp.where(use_up, stats[0][0], stats[1][0])
        total = jnp.where(use_up, stats[0][1], stats[1][1])
        zstat[c] = join_stats(top, total, scales)

        def split_one(zz, _, c=c):
            rows = values[:, pl.ds(pl.multiple_of(zz * 8, 8), 8), :]
            rows = rows.reshape(2 * HALF * 8, LAT)
            zcodes[c, zz] = rows.astype(jnp.int32).astype(jnp.int16)
            return 0

        lax.fori_loop(0, RING_Z, split_one, 0)
        for k in (4, 3, 5, 2, 6, 1, 7):
            there = (z + k) % RING_Z
            back = RING_Z - k
            index = 2 * (c * RING_Z + k)
            arrivals[c, k] = (
                push(
                    zstat.at[c, pl.ds(there * 8, 8)], zstat_in.at[c, k], send_z, recv_z, index + 1,
                    at(there, y),
                ),
                push(zcodes.at[c, there], zin.at[c, k], send_z, recv_z, index, at(there, y)),
            )

    for c in range(CHUNKS):
        for k in range(1, RING_Z):
            for copy in arrivals[c, k]:
                copy.wait_recv()
        blocks = [zstat[c, pl.ds(pl.multiple_of(z * 8, 8), 8), :]]
        blocks = blocks + [zstat_in[c, k] for k in range(1, RING_Z)]
        top, total, weights = merge_stats(blocks)
        for way in range(2):
            sums = []
            for i in range(HALF):
                j = 6 * way + HALF * c + i
                sums.append(1.0 / column(total, j))
            mixed = None
            for k in range(RING_Z):
                codes = zcodes.at[c, z] if k == 0 else zin.at[c, k]
                part = decode(codes[...])[way * HALF * 8 : (way + 1) * HALF * 8]
                factor = jnp.concatenate(
                    [column(weights[k], 6 * way + HALF * c + i) * sums[i] for i in range(HALF)], axis=0
                )
                mixed = part * factor if mixed is None else mixed + part * factor
            first = (6 * way + HALF * c) * 8
            out_ref[first : first + HALF * 8, :] = mixed
    for copy in copies:
        copy.wait_send()


def merge_over_owners(o_codes, ml):
    half = (2, CHUNKS, HALF, 64, LAT)
    vmem = pl.BlockSpec(memory_space=pltpu.VMEM)
    return pl.pallas_call(
        merge_kernel,
        out_shape=jax.ShapeDtypeStruct((96, LAT), jnp.float32),
        in_specs=[vmem, vmem],
        out_specs=vmem,
        scratch_shapes=[
            pltpu.VMEM(half, jnp.int16),
            pltpu.VMEM(half, jnp.int16),
            pltpu.VMEM(half, jnp.int16),
            pltpu.VMEM(half, jnp.int16),
            pltpu.VMEM((4, 64, 128), jnp.float32),
            pltpu.VMEM((2, CHUNKS, 64, 128), jnp.float32),
            pltpu.VMEM((2, CHUNKS, 64, 128), jnp.float32),
            pltpu.VMEM((CHUNKS, RING_Z, 16 * HALF, LAT), jnp.int16),
            pltpu.VMEM((CHUNKS, RING_Z, 16 * HALF, LAT), jnp.int16),
            pltpu.VMEM((CHUNKS, 64, 128), jnp.float32),
            pltpu.VMEM((CHUNKS, RING_Z, 8, 128), jnp.float32),
            pltpu.VMEM((2 * HALF, 64, LAT), jnp.float32),
            pltpu.SemaphoreType.DMA((4 + 8 * CHUNKS,)),
            pltpu.SemaphoreType.DMA((4 + 8 * CHUNKS,)),
            pltpu.SemaphoreType.DMA((2 * CHUNKS * RING_Z,)),
            pltpu.SemaphoreType.DMA((2 * CHUNKS * RING_Z,)),
        ],
        compiler_params=pltpu.CompilerParams(
            vmem_limit_bytes=VMEM_LIMIT, collective_id=1, has_side_effects=True
        ),
        cost_estimate=pl.CostEstimate(
            flops=20_000_000, bytes_accessed=100_000_000, transcendentals=0
        ),
        name="merge_over_owners",
    )(o_codes, ml)


def gather_kernel(
    served_ref, q_ref, lat_ref, out_ref, lat_out_ref,
    xbuf, lbuf, chosen,
    send_x, recv_x, send_sem, recv_sem, local_sem,
):
    role = lax.axis_index("role")
    group = lax.axis_index("grp")
    me = lax.axis_index("dev")
    z = me // RING_Y
    y = me % RING_Y

    def at(zz, yy):
        return (role, group, zz * RING_Y + yy)

    neighbours = {
        "up": at(z, (y + 1) % RING_Y),
        "down": at(z, (y + 3) % RING_Y),
        "in": at((z + 1) % RING_Z, y),
        "out": at((z + 7) % RING_Z, y),
    }
    greet(list(neighbours.values()) + [(role, (group + k) % 4, me) for k in range(1, 4)])
    copies = []
    arriving = []
    for k in (2, 1, 3):
        target = (role, (group + k) % 4, me)
        for src, buf, index in ((q_ref, xbuf, 2 * k), (lat_ref, lbuf, 2 * k + 1)):
            copy = pltpu.make_async_remote_copy(
                src_ref=src, dst_ref=buf.at[group], send_sem=send_x.at[index],
                recv_sem=recv_x.at[index], device_id=target, device_id_type=MESH_IDS,
            )
            copy.start()
            copies.append(copy)
            arriving.append(copy)
    xbuf[group] = q_ref[...]
    lbuf[group] = lat_ref[...]
    for copy in arriving:
        copy.wait_recv()

    def pick(index):
        pair = xbuf[index // 12, (index % 12) // 2].astype(jnp.float32)
        return jnp.where(index % 2 == 0, pair[:8], pair[8:])

    for p in range(6):
        both = jnp.concatenate([pick(served_ref[2 * p]), pick(served_ref[2 * p + 1])], axis=0)
        chosen[16 * p : 16 * p + 16, :] = both.astype(jnp.bfloat16)
    mine = served_ref[jnp.minimum(me, 11)]
    lat_out_ref[...] = lbuf[mine // 12, (mine % 12) // 4]

    def slot(dz, dy):
        return ((z - dz + 2 * RING_Z) % RING_Z) * RING_Y + (y - dy + 2 * RING_Y) % RING_Y

    local = pltpu.make_async_copy(chosen, out_ref.at[me], local_sem)
    local.start()
    waits = {}

    def send(half, dz, dy, to):
        rows = pl.ds(48 * half, 48)
        place = slot(dz, dy)
        source = chosen.at[rows] if (dz, dy) == (0, 0) else out_ref.at[place, rows]
        ndz, ndy = dz, dy
        if to == "in":
            ndz = dz + 1
        if to == "out":
            ndz = dz - 1
        if to == "up":
            ndy = dy + 1
        if to == "down":
            ndy = dy - 1
        index = half * 32 + (ndz % RING_Z) * RING_Y + ndy % RING_Y
        copy = pltpu.make_async_remote_copy(
            src_ref=source, dst_ref=out_ref.at[place, rows], send_sem=send_sem.at[index],
            recv_sem=recv_sem.at[index], device_id=neighbours[to], device_id_type=MESH_IDS,
        )
        copy.start()
        copies.append(copy)
        here = out_ref.at[slot(ndz, ndy), rows]
        waits[half, ndz, ndy] = pltpu.make_async_remote_copy(
            src_ref=here, dst_ref=here, send_sem=send_sem.at[index],
            recv_sem=recv_sem.at[index], device_id=neighbours[to], device_id_type=MESH_IDS,
        )
        return (half, ndz, ndy)

    def z_steps(half, dz, dy):
        deep = 4 if (half == 0 or dy in (0, 1)) else 3
        steps = []
        if 0 <= dz < deep:
            steps.append("in")
        if 0 >= dz > deep - 7:
            steps.append("out")
        return steps

    def y_steps(half, dz, dy):
        if dy == 0:
            return ["up", "down"]
        if dy == 1 and (half == 1 or dz % 2 == 0):
            return ["up"]
        if dy == -1 and half == 0 and dz % 2 == 1:
            return ["down"]
        return []

    def forward(block):
        half, dz, dy = block
        steps = []
        if half == 0:
            steps = (z_steps(half, dz, dy) if dy == 0 else []) + y_steps(half, dz, dy)
        else:
            steps = (y_steps(half, dz, dy) if dz == 0 else []) + z_steps(half, dz, dy)
        return [send(half, dz, dy, to) for to in steps]

    frontier = forward((0, 0, 0)) + forward((1, 0, 0))
    while frontier:
        later = []
        for block in frontier:
            waits[block].wait_recv()
            later = later + forward(block)
        frontier = later
    local.wait()
    for copy in copies:
        copy.wait_send()


def gather_queries(served, queries, latents):
    vmem = pl.BlockSpec(memory_space=pltpu.VMEM)
    return pl.pallas_call(
        gather_kernel,
        out_shape=(
            jax.ShapeDtypeStruct((OWNERS, 96, KDIM), jnp.bfloat16),
            jax.ShapeDtypeStruct((16, KDIM), jnp.bfloat16),
        ),
        in_specs=[pl.BlockSpec(memory_space=pltpu.SMEM), vmem, vmem],
        out_specs=(pl.BlockSpec(memory_space=pl.ANY), vmem),
        scratch_shapes=[
            pltpu.VMEM((4, 6, 16, KDIM), jnp.bfloat16),
            pltpu.VMEM((4, 3, 16, KDIM), jnp.bfloat16),
            pltpu.VMEM((96, KDIM), jnp.bfloat16),
            pltpu.SemaphoreType.DMA((8,)),
            pltpu.SemaphoreType.DMA((8,)),
            pltpu.SemaphoreType.DMA((64,)),
            pltpu.SemaphoreType.DMA((64,)),
            pltpu.SemaphoreType.DMA,
        ],
        compiler_params=pltpu.CompilerParams(
            vmem_limit_bytes=VMEM_LIMIT, collective_id=2, has_side_effects=True
        ),
        cost_estimate=pl.CostEstimate(
            flops=1_000_000, bytes_accessed=80_000_000, transcendentals=0
        ),
        name="gather_queries",
    )(served, queries, latents)


def per_device(
    pool_pages,
    kv_gain,
    queries,
    decode_latent,
    served_request,
    resident_pages,
    resident_tail,
    page_dest,
):
    role = lax.axis_index("role")
    group = lax.axis_index("grp")
    owner = lax.axis_index("dev")
    at_prefill = role == 0
    own = pool_pages[0, 0, 0]
    pages_dev = own.shape[0]
    swap = [(0, 1), (1, 0)]
    partner = lax.ppermute(own, "role", swap)

    counts = resident_pages[0]
    tail_len = resident_tail[0]
    req_grp = counts.shape[0]
    per_prompt = pages_dev // req_grp
    res_len = PAGE * (counts - 1) + tail_len
    page_ids = jnp.arange(pages_dev, dtype=jnp.int32)
    positions = (
        res_len[page_ids // per_prompt][:, None]
        + ((owner * per_prompt + page_ids % per_prompt) * PAGE)[:, None]
        + jnp.arange(PAGE, dtype=jnp.int32)[None, :]
    )
    targets = lax.dynamic_index_in_dim(page_dest[0], owner, 0, keepdims=False)
    wanted = jnp.arange(OWNERS, dtype=jnp.int32) * 2 + role
    hits = targets[None, :] == wanted[:, None]
    inverse = jnp.max(jnp.where(hits, page_ids[None, :], -1), axis=1).astype(jnp.int32)
    role_arr = role.astype(jnp.int32).reshape(1)
    fresh, resident, outgoing = finish_and_pack(
        inverse, role_arr, own, partner, kv_gain, rope_table(positions)
    )
    routed = lax.all_to_all(outgoing, "dev", split_axis=0, concat_axis=0, tiled=True)
    routed_other = lax.ppermute(routed, "role", swap)
    received = jnp.stack(
        [jnp.where(at_prefill, routed, routed_other), jnp.where(at_prefill, routed_other, routed)],
        axis=1,
    ).reshape(2 * OWNERS, PAGE, KDIM)

    run_ends = jnp.cumsum(counts)
    starts = run_ends - counts
    flat = page_ids * OWNERS + owner
    begin = jnp.sum((flat[None, :] < starts[:, None]).astype(jnp.int32), axis=1)
    end = jnp.sum((flat[None, :] < run_ends[:, None]).astype(jnp.int32), axis=1)
    res_req = jnp.sum((flat[:, None] >= run_ends[None, :]).astype(jnp.int32), axis=1)
    valid = jnp.where(flat - starts[res_req] < counts[res_req] - 1, PAGE, tail_len[res_req])

    heads_here = queries.shape[2]
    steps = queries.shape[1]
    rows_here = steps * heads_here
    serving = lax.dynamic_slice_in_dim(served_request, group * req_grp, req_grp)
    q_all, latents = gather_queries(
        serving, queries.reshape(6, 16, KDIM), decode_latent.reshape(3, 16, KDIM)
    )
    mine = jnp.minimum(owner, req_grp - 1)
    own_latent = lax.dynamic_slice_in_dim(latents, (serving[mine] % 4) * steps, steps)
    new_positions = res_len[mine] + per_prompt * PAGE * OWNERS + jnp.arange(steps, dtype=jnp.int32)
    newk = finish_keys(own_latent, kv_gain, new_positions)
    newk = jnp.pad(newk, ((0, 2 * PAGE - steps), (0, 0)))

    o_part, ml = attend(
        begin, end, valid.astype(jnp.int32), owner.astype(jnp.int32).reshape(1),
        q_all, fresh, resident, newk,
    )
    merged = merge_over_owners(o_part, ml.reshape(RING_Y, 2 * OWNERS, 128))
    attention = merged.astype(jnp.bfloat16)
    attention = attention.reshape(req_grp, steps, heads_here, LAT)
    return (attention, received[None, None])


def solution(mesh):
    in_specs = (
        P("role", "grp", "dev", None, None, None),
        P(),
        P("grp", None, ("role", "dev"), None),
        P("grp", None, None),
        P(),
        P("grp", None),
        P("grp", None),
        P("grp", None, None),
    )
    out_specs = (P("grp", None, ("role", "dev"), None), P("grp", "dev", None, None, None))
    return jax.shard_map(
        per_device, mesh=mesh, in_specs=in_specs, out_specs=out_specs, check_vma=False
    )
```

time: 613 us -> 221 us (0.36)
  waiting for transfers between devices: 268 us -> 0.01 us
  other arithmetic: 151 us -> 9.7 us
  Pallas kernels: 0 us -> 119 us
  local copies, waits for them, and re-layouts: 68.8 us -> 13.4 us
  blocking collectives: 25.7 us -> 74.2 us
  matrix products: 46 us -> 0 us
  starting transfers between devices: 36 us -> 0.1 us
  between operations: 14.4 us -> 3.44 us
    all_to_all x4 -> x0, waiting for transfers between devices: 268 us -> none  [the longest x1 135 us: per_device(): lax.all_to_all(out_heads, 'dev', split_axis=2, concat_axis=0, tiled=True)]
    pallas_call x0 -> x4, Pallas kernels: none -> 119 us  [the longest x1 44.6 us: merge_over_owners(): pl.pallas_call(merge_kernel, out_shape=jax.ShapeDtypeStruct((96, LAT), jn...]
    scatter-add x8 -> x0, other arithmetic: 102 us -> none  [the longest x4 98.7 us: page_step(): (running_out * carry_over[..., None]).at[block_req]]
    all_to_all x0 -> x1, blocking collectives: none -> 74.2 us  [per_device(): lax.all_to_all(outgoing, 'dev', split_axis=0, concat_axis=0, tiled=True)]
    dot_general x10 -> x0, matrix products: 46 us -> none  [the longest x4 23.4 us: page_step(): jnp.einsum('btq,btc->bqc', unnormed.astype(jnp.bfloat16), block_of_keys[....]
    all_to_all x4 -> x0, starting transfers between devices: 35.4 us -> none  [the longest x1 11.8 us: per_device(): lax.all_to_all(outgoing, 'dev', split_axis=0, concat_axis=0, tiled=True)]
    gather x13 -> x2, local copies, waits for them, and re-layouts: 34.6 us -> 1.39 us  [the longest x1 0.7 us: per_device(): res_len[page_ids // per_prompt][:, None]]
    all_gather x2 -> x0, blocking collectives: 25.7 us -> none  [the longest x1 13 us: per_device(): lax.all_gather(queries, 'grp', axis=0, tiled=True)]
  transfers between devices with their start and end apart: 7 -> 2, of which waited for: 3 -> 0; matrix products, arithmetic and copies ran while one was open for 4% -> 5% of each run, Pallas kernels for 0% -> 51%
where the time goes in v1:
time: 221 us; the launch traced here: 220 us
  Pallas kernels  119 us (54%)
  blocking collectives  74.2 us (34%)
  local copies, waits for them, and re-layouts  13.4 us (6%)
  other arithmetic  9.7 us (4%)
  between operations  3.44 us (2%)
    all_to_all x1, blocking collectives, per_device(): lax.all_to_all(outgoing, 'dev', split_axis=0, concat_axis=0, tiled=True)  74.2 us
    pallas_call x1, Pallas kernels, merge_over_owners(): pl.pallas_call(merge_kernel, out_shape=jax.ShapeDtypeStruct((96, LAT), jn...  44.6 us
    pallas_call x1, Pallas kernels, gather_queries(): pl.pallas_call(gather_kernel, out_shape=(jax.ShapeDtypeStruct((OWNERS, 96...  44.1 us
    pallas_call x1, Pallas kernels, attend(): pl.pallas_call(attend_kernel, grid=(pairs,), out_shape=(jax.ShapeDtypeStr...  23.1 us
    pallas_call x1, Pallas kernels, finish_and_pack(): pl.pallas_call(finish_kernel, out_shape=(page, page, jax.ShapeDtypeStruct...  7.01 us
    unnamed x22, local copies, waits for them, and re-layouts  5.39 us
  transfers between devices with their start and end apart: 2, of which 0 were waited for; matrix products, arithmetic and copies ran while one was open for 5% of the time, Pallas kernels for 51%

profile of v1, /device:TPU:16, one launch (start us, length us, event | category | flops | bytes accessed | tf_op | source)
XLA Modules:
  0.0 219.7 jit_solution(8430177524172876272)
XLA Ops:
  0.6 0.0 copy-start
  0.6 0.1 collective-permute-start
  0.8 0.8 reduce-window.7
  1.6 0.1 convert_reduce_fusion
  1.7 0.7 multiply_add_fusion
  2.4 0.7 gather_fusion.3
  3.1 0.0 copy-done
  3.1 0.2 dynamic-slice_reduce_fusion
  3.3 0.1 select_reduce_fusion.inverse_ref
  3.4 0.1 add_convert_fusion
  3.5 2.8 %multiply_cosine_fusion = (f32[24,64,32]{2,1,0:T(8,128)S(1)}, f32[24,64,32]{2,1,0:T(8,128)S(1)}, f32[24,64,32]{2,1,0:T(8,128)S(1)}) fusion(f32[32]{0:T(128)S(1)} %multiply_power_fusion, f32[24,64]{1,0:T(8,128)S(1)} %add_convert_fusion), kind=kLoop, calls=%fused_computation.8 | loop fusion | flops 98304 | bytes 596096 | tf_op jit(solution)/shard_map/cos | solution.py:49
  6.3 0.7 pad_maximum_fusion.1.table_ref
  7.0 0.0 collective-permute-done.partner_ref
  7.0 0.0 copy-done.5
  7.0 7.0 %finish_and_pack.1 = (bf16[24,64,576]{2,1,0:T(8,128)(2,1)S(1)}, bf16[24,64,576]{2,1,0:T(8,128)(2,1)S(1)}, bf16[32,64,576]{2,1,0:T(8,128)(2,1)}) custom-call(s32[32]{0:T(128)S(1)} %select_reduce_fusion.inverse_ref, s32[1]{0:T(128)} %bitcast.7.role_ref, bf16[24,64,576]{2,1,0:T(8,128)(2,1)} %bitcast.33, bf16[24,64,576]{2,1,0:T(8,128)(2,1)} %collective-permute-done.partner_ref, ...), custom_call_target="tpu_custom_call" | custom-call | flops 20000000 | bytes 10000000 | tf_op jit(solution)/shard_map/finish_and_pack/pallas_call | solution.py:91
  14.0 0.0 copy-start.9
  14.0 0.0 copy-start.8
  14.1 74.2 %all_to_all.5 = bf16[32,64,576]{2,1,0:T(8,128)(2,1)} all-to-all(bf16[32,64,576]{2,1,0:T(8,128)(2,1)} %get-tuple-element.15), channel_id=1, replica_groups=mesh['role'=2,'grp'=4,'dev'=32] {'dev'}, dimensions={0} | all-to-all | bytes 4718592 | tf_op jit(solution)/shard_map/all_to_all | solution.py:652
  88.3 0.0 copy-done.3
  88.3 0.0 collective-permute-start.1
  88.3 0.0 copy-done.10
  88.3 0.6 dynamic_slice.21
  90.9 0.1 dynamic_slice.18.served_ref
  90.9 0.6 dynamic_slice.23
  91.5 0.7 gather_fusion
  92.2 0.0 copy-done.6
  92.2 0.7 gather_fusion.2
  92.9 0.0 copy-done.7
  92.9 0.7 gather_fusion.1
  93.6 0.0 copy-done.9
  93.7 0.1 reshape.197.q_ref
  94.4 44.1 %gather_queries.1 = (bf16[32,96,576]{2,1,0:T(8,128)(2,1)S(1)}, bf16[16,576]{1,0:T(8,128)(2,1)S(1)}) custom-call(s32[12]{0:T(128)S(1)} %dynamic_slice.18.served_ref, bf16[6,16,576]{2,1,0:T(8,128)(2,1)S(1)} %reshape.197.q_ref, bf16[3,16,576]{2,1,0:T(8,128)(2,1)S(1)} %reshape.198.lat_ref), custom_call_target="tpu_custom_call" | custom-call | flops 1000000 | bytes 80000000 | tf_op jit(solution)/shard_map/gather_queries/pallas_call | solution.py:586
  138.5 0.0 copy-start.1
  138.5 1.9 copy-done.1
  140.5 0.1 multiply_reduce_fusion
  140.6 0.2 convert_reduce_fusion.1
  140.8 0.1 fusion.11
  140.9 0.1 multiply_convert_fusion
  141.0 0.1 fusion.5.newk_ref
  141.1 1.5 copy-done.4
  142.6 23.1 %attend_pages.1 = (s16[4,12,64,512]{3,2,1,0:T(8,128)(2,1)}, f32[256,128]{1,0:T(8,128)S(1)}) custom-call(s32[12]{0:T(128)S(1)} %get-tuple-element.17.begin_ref, s32[12]{0:T(128)S(1)} %get-tuple-element.16.end_ref, s32[24]{0:T(128)S(1)} %compare_select_fusion.2.valid_ref, s32[1]{0:T(128)} %bitcast.6.owner_ref, bf16[32,96,576]{2,1,0:T(8,128)(2,1)} %copy-done.1, ...), custom_call_target="tpu_custom_call" | custom-call | flops 2000000000 | bytes 11000000 | tf_op jit(solution)/shard_map/attend_pages/pallas_call | solution.py:197
  165.7 1.9 copy-done.2
  167.6 44.6 %merge_over_owners.1 = f32[96,512]{1,0:T(8,128)S(1)} custom-call(s16[4,12,64,512]{3,2,1,0:T(8,128)(2,1)S(1)} %copy-done.2, f32[4,64,128]{2,1,0:T(8,128)S(1)} %bitcast.26), custom_call_target="tpu_custom_call" | custom-call | flops 20000000 | bytes 100000000 | tf_op jit(solution)/shard_map/merge_over_owners/pallas_call | solution.py:430
  212.2 0.7 reshape.202
  212.9 0.0 collective-permute-done.1
  212.9 3.0 %select_bitcast_fusion.1 = (bf16[32,1,64,576]{3,2,0,1:T(8,128)(2,1)S(1)}, bf16[32,1,64,576]{3,2,0,1:T(8,128)(2,1)S(1)}) fusion(bf16[32,64,576]{2,1,0:T(8,128)(2,1)} %all_to_all.5, bf16[32,64,576]{2,1,0:T(8,128)(2,1)} %collective-permute-done.1, pred[]{:T(512)S(6)} %eq.26), kind=kLoop, calls=%fused_computation.6 | loop fusion | flops 2359296 | bytes 9437185 | tf_op jit(solution)/shard_map/stack | solution.py:654
  215.9 0.8 pad_maximum_fusion
  216.7 3.0 %copy.11 = bf16[32,2,64,576]{3,2,1,0:T(8,128)(2,1)} copy(bf16[32,2,64,576]{3,2,0,1:T(8,128)(2,1)S(1)} %pad_maximum_fusion) | data formatting | bytes 9437184 | tf_op jit(solution)/shard_map/stack | solution.py:654
  (21 shorter events, 0.1 us)
Async XLA Ops:
  0.6 2.5 %copy-start = (s32[1,32,24]{1,2,0:T(8,128)S(1)}, s32[1,32,24]{1,2,0:T(8,128)}, u32[]{:S(2)}) copy-start(s32[1,32,24]{1,2,0:T(8,128)} %param.15) | copy-start | bytes 9220
  0.6 6.3 %collective-permute-start = (bf16[24,64,576]{2,1,0:T(8,128)(2,1)}, bf16[24,64,576]{2,1,0:T(8,128)(2,1)}, u32[]{:S(2)}, u32[]{:S(2)}) collective-permute-start(bf16[24,64,576]{2,1,0:T(8,128)(2,1)} %bitcast.32), channel_id=1, source_target_pairs={{0,128},{128,0},{1,129},{129,1},{2,130},{130,2},{3,131},{131,3},{4... | collective-permute-start | bytes 5308424 | tf_op jit(solution)/shard_map/ppermute | solution.py:631
  3.5 3.5 %copy-start.5 = (f32[512]{0:T(512)S(1)}, f32[512]{0:T(512)}, u32[]{:S(2)}) copy-start(f32[512]{0:T(512)} %param.9) | copy-start | bytes 6148
  14.0 74.3 %copy-start.3 = (bf16[24,64,576]{2,1,0:T(8,128)(2,1)}, bf16[24,64,576]{2,1,0:T(8,128)(2,1)S(1)}, u32[]{:S(2)}) copy-start(bf16[24,64,576]{2,1,0:T(8,128)(2,1)S(1)} %get-tuple-element.11.resident_ref) | copy-start | bytes 5308420
  14.0 74.3 %copy-start.10 = (s32[48]{0:T(128)S(1)}, s32[48]{0:T(128)}, u32[]{:S(2)}) copy-start(s32[48]{0:T(128)} %param.12) | copy-start | bytes 580
  14.0 78.2 %copy-start.6 = (s32[1,12]{1,0:T(1,128)S(1)}, s32[1,12]{1,0:T(1,128)}, u32[]{:S(2)}) copy-start(s32[1,12]{1,0:T(1,128)} %param.14) | copy-start | bytes 148
  14.0 78.9 %copy-start.7 = (s32[1,12]{1,0:T(1,128)S(1)}, s32[1,12]{1,0:T(1,128)}, u32[]{:S(2)}) copy-start(s32[1,12]{1,0:T(1,128)} %param.13) | copy-start | bytes 148
  14.0 79.6 %copy-start.9 = (bf16[12,4,576]{2,1,0:T(4,128)(2,1)S(1)}, bf16[12,4,576]{2,1,0:T(4,128)(2,1)}, u32[]{:S(2)}) copy-start(bf16[12,4,576]{2,1,0:T(4,128)(2,1)} %param.11) | copy-start | bytes 165892
  14.0 79.6 %copy-start.8 = (bf16[12,4,2,576]{3,2,1,0:T(2,128)(2,1)S(1)}, bf16[12,4,2,576]{3,2,1,0:T(2,128)(2,1)}, u32[]{:S(2)}) copy-start(bf16[12,4,2,576]{3,2,1,0:T(2,128)(2,1)} %param.10) | copy-start | bytes 331780
  88.3 124.6 %collective-permute-start.1 = (bf16[32,64,576]{2,1,0:T(8,128)(2,1)}, bf16[32,64,576]{2,1,0:T(8,128)(2,1)}, u32[]{:S(2)}, u32[]{:S(2)}) collective-permute-start(bf16[32,64,576]{2,1,0:T(8,128)(2,1)} %all_to_all.5), channel_id=1, source_target_pairs={{0,128},{128,0},{1,129},{129,1},{2,130},{130,2},{3,131},{131,3},{4... | collective-permute-start | bytes 7077896 | tf_op jit(solution)/shard_map/ppermute | solution.py:653
  138.5 1.9 copy-start.1
  141.1 1.5 copy-start.4
  165.7 1.9 copy-start.2

commit v2 on v0

v2 whole, which is shorter than its diff:
```python
import functools

import jax
import jax.numpy as jnp
from jax import lax
from jax.experimental import pallas as pl
from jax.experimental.pallas import tpu as pltpu
from jax.sharding import PartitionSpec as P

logit_scale_factor = 192.0 ** (-0.5)
epsilon = 1e-06
lowest = -1e30

VMEM_LIMIT = 58 * 1024 * 1024
LAT = 512
KDIM = 576
PAGE = 64
OWNERS = 32
RING_Y = 4
RING_Z = 8


SERVED, BEGIN, END, REQUEST, VALID, SAME, INVERSE = 0, 12, 24, 36, 60, 84, 108


def rope_table(positions):
    lane = jnp.arange(128)
    frequency = 10000.0 ** (-(lane % 32).astype(jnp.float32) / 32)
    angles = positions[..., None].astype(jnp.float32) * frequency
    sine_part = jnp.sin(angles)
    turned = jnp.where(lane < 96, -sine_part, sine_part)
    return jnp.where(lane < 64, jnp.cos(angles), turned)


MESH_IDS = pl.DeviceIdType.MESH
CODE_TOP = 32767.0
CHUNKS = 2
HALF = 6 // CHUNKS


DISTANCES = [(0, dy) for dy in (2, 1, 3)]
DISTANCES = DISTANCES + [(dz, dy) for dy in (1, 3, 2, 0) for dz in (4, 3, 5, 2, 6, 1, 7)]
DISTANCES = DISTANCES + [(0, 0)]
EARLY, BEFORE_ATTENTION = 6, 20


def everyone(role, group, z, y):
    return [
        (role, group, ((z + dz) % RING_Z) * RING_Y + (y + dy) % RING_Y)
        for dz, dy in DISTANCES
        if (dz, dy) != (0, 0)
    ]


def greet(devices):
    barrier = pltpu.get_barrier_semaphore()
    for device in devices:
        pl.semaphore_signal(barrier, inc=1, device_id=device, device_id_type=MESH_IDS)
    pl.semaphore_wait(barrier, len(devices))


def merge_stats(blocks):
    lane = lax.broadcasted_iota(jnp.int32, blocks[0].shape, 1)
    top = functools.reduce(jnp.maximum, blocks)
    total = jnp.zeros_like(top)
    weights = []
    for block in blocks:
        part = jnp.exp(jnp.where(lane < 16, block - top, 0.0))
        total = total + part * pltpu.roll(block, 112, 1)
        weights.append(part * pltpu.roll(block, 96, 1))
    return top, total, weights


def column(block, index):
    lane = lax.broadcasted_iota(jnp.int32, block.shape, 1)
    return jnp.sum(jnp.where(lane == index, block, 0.0), axis=1, keepdims=True)


def encode(values):
    scale = jnp.max(jnp.abs(values), axis=1, keepdims=True)
    codes = jnp.floor(values * (CODE_TOP / jnp.maximum(scale, 1e-30)) + 0.5)
    return codes.astype(jnp.int32).astype(jnp.int16), scale * (1.0 / CODE_TOP)


def decode(codes):
    return codes.astype(jnp.int32).astype(jnp.float32)


def join_stats(top, total, scales):
    lane = lax.broadcasted_iota(jnp.int32, top.shape, 1)
    return jnp.where(lane < 16, top, jnp.where(lane < 32, pltpu.roll(total, 16, 1), scales))


def decode_kernel(
    meta_ref, q_ref, lat_ref, own_ref, gain_ref, table_ref, newtable_ref,
    out_ref, cache_ref,
    xbuf, lbuf, q_all, q_rows, partner, fresh, outgoing,
    states, state_stats, o_codes, stats,
    relay_in, direct_in, merged, merged_in, stat_in, mstat, mstat_in,
    zcodes, zin, zstat, zstat_in, values, out_f32,
    send_x, recv_x, send_q, recv_q, send_page, recv_page, send_role, recv_role,
    send_y, recv_y, send_z, recv_z, local_sem,
):
    role = lax.axis_index("role")
    group = lax.axis_index("grp")
    me = lax.axis_index("dev")
    z = me // RING_Y
    y = me % RING_Y
    up = (y + 1) % RING_Y
    down = (y + 3) % RING_Y
    far = (y + 2) % RING_Y
    rows = 8 * OWNERS
    pages = own_ref.shape[0]
    at_prefill = role == 0

    def at(zz, yy):
        return (role, group, zz * RING_Y + yy)

    other_core = (1 - role, group, me)
    neighbours = {
        "up": at(z, up),
        "down": at(z, down),
        "in": at((z + 1) % RING_Z, y),
        "out": at((z + 7) % RING_Z, y),
    }
    shards = [(role, (group + k) % 4, me) for k in range(1, 4)]
    greet(everyone(role, group, z, y) + shards + [other_core])
    copies = []

    def push(src, dst, sends, recvs, index, target):
        copy = pltpu.make_async_remote_copy(
            src_ref=src, dst_ref=dst, send_sem=sends.at[index], recv_sem=recvs.at[index],
            device_id=target, device_id_type=MESH_IDS,
        )
        copy.start()
        copies.append(copy)
        return copy

    arriving, arriving_latents = [], []
    for k in (2, 1, 3):
        target = (role, (group + k) % 4, me)
        arriving.append(push(q_ref, xbuf.at[group], send_x, recv_x, 2 * k, target))
    exchange = push(own_ref, partner, send_role, recv_role, OWNERS, other_core)
    for k in (2, 1, 3):
        target = (role, (group + k) % 4, me)
        arriving_latents.append(push(lat_ref, lbuf.at[group], send_x, recv_x, 2 * k + 1, target))
    xbuf[group] = q_ref[...]
    lbuf[group] = lat_ref[...]
    for copy in arriving:
        copy.wait_recv()

    def served(j):
        return meta_ref[SERVED + j]

    def pick(index):
        pair = xbuf[index // 12, (index % 12) // 2].astype(jnp.float32)
        return jnp.where(index % 2 == 0, pair[:8], pair[8:])

    for p in range(6):
        both = jnp.concatenate([pick(served(2 * p)), pick(served(2 * p + 1))], axis=0)
        q_all[me, 16 * p : 16 * p + 16, :] = both.astype(jnp.bfloat16)

    def slot(dz, dy):
        return ((z - dz + 2 * RING_Z) % RING_Z) * RING_Y + (y - dy + 2 * RING_Y) % RING_Y

    waits = {}

    def send(half, dz, dy, to):
        span = pl.ds(48 * half, 48)
        place = slot(dz, dy)
        ndz = dz + {"in": 1, "out": -1}.get(to, 0)
        ndy = dy + {"up": 1, "down": -1}.get(to, 0)
        index = half * 32 + (ndz % RING_Z) * RING_Y + ndy % RING_Y
        block = q_all.at[place, span]
        push(block, block, send_q, recv_q, index, neighbours[to])
        here = q_all.at[slot(ndz, ndy), span]
        waits[half, ndz, ndy] = pltpu.make_async_remote_copy(
            src_ref=here, dst_ref=here, send_sem=send_q.at[index], recv_sem=recv_q.at[index],
            device_id=neighbours[to], device_id_type=MESH_IDS,
        )
        return (half, ndz, ndy)

    def z_steps(half, dz, dy):
        deep = 4 if (half == 0 or dy in (0, 1)) else 3
        steps = []
        if 0 <= dz < deep:
            steps.append("in")
        if 0 >= dz > deep - 7:
            steps.append("out")
        return steps

    def y_steps(half, dz, dy):
        if dy == 0:
            return ["up", "down"]
        if dy == 1 and (half == 1 or dz % 2 == 0):
            return ["up"]
        if dy == -1 and half == 0 and dz % 2 == 1:
            return ["down"]
        return []

    def forward(block):
        half, dz, dy = block
        if half == 0:
            steps = (z_steps(half, dz, dy) if dy == 0 else []) + y_steps(half, dz, dy)
        else:
            steps = (y_steps(half, dz, dy) if dz == 0 else []) + z_steps(half, dz, dy)
        return [send(half, dz, dy, to) for to in steps]

    def advance(frontier):
        later = []
        for block in frontier:
            waits[block].wait_recv()
            later = later + forward(block)
        return later

    frontier = forward((0, 0, 0)) + forward((1, 0, 0))

    exchange.wait_recv()
    gain = gain_ref[...]

    def finish(raw, table):
        latent = raw[:, :LAT]
        mean_square = jnp.sum(latent * latent, axis=-1, keepdims=True) * (1.0 / LAT)
        normed = latent * lax.rsqrt(mean_square + epsilon) * gain
        rope = raw[:, LAT:]
        swapped = jnp.concatenate([rope[:, 32:], rope[:, :32]], axis=-1)
        turned = rope * table[:, :64] + swapped * table[:, 64:]
        return jnp.concatenate([normed, turned], axis=-1).astype(jnp.bfloat16)

    def one_page(i, _):
        raw = jnp.where(at_prefill, own_ref[i], partner[i]).astype(jnp.float32)
        fresh[i] = finish(raw, table_ref[i])
        return 0

    third = pages // 3
    for part in range(3):
        lax.fori_loop(part * third, (part + 1) * third, one_page, 0)
        if part < 2:
            frontier = advance(frontier)

    def one_slot(t, _):
        page = meta_ref[INVERSE + t]
        found = fresh[jnp.maximum(page, 0)]
        outgoing[t] = jnp.where(page >= 0, found, jnp.zeros_like(found))
        return 0

    lax.fori_loop(0, OWNERS, one_slot, 0)
    frontier = advance(frontier)

    sent_pages = DISTANCES[:-1]
    landing = []
    over = []

    def send_pages(first, last):
        for i in range(first, last):
            dz, dy = sent_pages[i]
            there = ((z + dz) % RING_Z) * RING_Y + (y + dy) % RING_Y
            landing.append(
                push(
                    outgoing.at[there], cache_ref.at[me, role], send_page, recv_page, i,
                    (role, group, there),
                )
            )

    def hand_over(first, last):
        for i in range(first, last):
            dz, dy = sent_pages[i]
            landing[i].wait_recv()
            page = cache_ref.at[slot(dz, dy), role]
            over.append(push(page, page, send_role, recv_role, i, other_core))

    send_pages(0, EARLY)
    keep_own = pltpu.make_async_copy(outgoing.at[me], cache_ref.at[me, role], local_sem)
    keep_own.start()
    over.append(
        push(outgoing.at[me], cache_ref.at[me, role], send_role, recv_role, OWNERS - 1, other_core)
    )
    while frontier:
        frontier = advance(frontier)
    send_pages(EARLY, BEFORE_ATTENTION)

    def order_rows(p, _):
        for yy in range(RING_Y):
            blocks = [
                q_all[zz * RING_Y + yy, pl.ds(pl.multiple_of(16 * p, 16), 16), :].astype(jnp.float32)
                for zz in range(RING_Z)
            ]
            for jj in range(2):
                picked = jnp.concatenate([block[jj * 8 : jj * 8 + 8] for block in blocks], axis=0)
                q_rows[2 * p + jj, yy * 64 : yy * 64 + 64, :] = picked.astype(jnp.bfloat16)
        return 0

    lax.fori_loop(0, 6, order_rows, 0)

    lane = lax.broadcasted_iota(jnp.int32, (rows, 2 * PAGE), 1)
    low = lane < PAGE
    step_of_row = (lax.broadcasted_iota(jnp.int32, (rows, 2 * PAGE), 0) % 8) // 2

    def score(q, keys):
        s = lax.dot_general(q, keys, (((1,), (1,)), ((), ())), preferred_element_type=jnp.float32)
        return s * logit_scale_factor

    states[0] = jnp.zeros((rows, LAT), jnp.float32)
    state_stats[0] = jnp.zeros((rows, 2), jnp.float32)
    page_lane = lax.broadcasted_iota(jnp.int32, (rows, PAGE), 1)

    def page_terms(x):
        request = meta_ref[REQUEST + x]
        keys = jnp.where(at_prefill, partner[x], own_ref[x])
        visible = page_lane < meta_ref[VALID + x]
        s = jnp.where(visible, score(q_rows[request], keys), lowest)
        m = jnp.max(s, axis=1, keepdims=True)
        e = jnp.where(visible, jnp.exp(s - m), 0.0)
        l = jnp.sum(e, axis=1, keepdims=True)
        o = jnp.dot(e.astype(jnp.bfloat16), keys[:, :LAT], preferred_element_type=jnp.float32)
        return m, l, o

    def chain(x, terms):
        m, l, o = terms
        same = meta_ref[SAME + x] == 1
        before = state_stats[x]
        m_before = jnp.where(same, before[:, 0:1], lowest)
        m_now = jnp.maximum(m, m_before)
        carry = jnp.where(same, jnp.exp(m_before - m_now), 0.0)
        f = jnp.exp(m - m_now)
        l_now = before[:, 1:2] * carry + l * f
        state_stats[x + 1] = jnp.concatenate([m_now, l_now], axis=1)
        states[x + 1] = states[x] * carry + o * f

    def two_resident(i, _):
        terms = [page_terms(2 * i), page_terms(2 * i + 1)]
        chain(2 * i, terms[0])
        chain(2 * i + 1, terms[1])
        return 0

    lax.fori_loop(0, pages // 2, two_resident, 0)

    for copy in arriving_latents:
        copy.wait_recv()

    mine = served(jnp.minimum(me, 11))
    new_raw = lbuf[mine // 12, (mine % 12) // 4].astype(jnp.float32)
    new_keys = finish(new_raw, newtable_ref[...])
    new_keys = jnp.concatenate(
        [new_keys, jnp.zeros((2 * PAGE - 16, KDIM), jnp.bfloat16)], axis=0
    )
    new_visible = (lane // 4 == mine % 4) & (lane % 4 <= step_of_row)

    def weigh(q, keys):
        s = score(q, keys)
        m1 = jnp.max(jnp.where(low, s, lowest), axis=1, keepdims=True)
        m2 = jnp.max(jnp.where(low, lowest, s), axis=1, keepdims=True)
        mb = jnp.where(low, m1, m2)
        e = jnp.exp(s - mb)
        m_now = jnp.maximum(m1, m2)
        f = jnp.exp(mb - m_now)
        l = jnp.sum(e * f, axis=1, keepdims=True)
        wide = e.astype(jnp.bfloat16).astype(jnp.float32) * f
        hi = wide.astype(jnp.bfloat16)
        lo = (wide - hi.astype(jnp.float32)).astype(jnp.bfloat16)
        v = keys[:, :LAT]
        o = jnp.dot(
            jnp.concatenate([hi, lo], axis=1),
            jnp.concatenate([v, v], axis=0),
            preferred_element_type=jnp.float32,
        )
        return m_now, l, o

    def whole_request(c, j):
        keys = fresh[pl.ds(2 * j, 2)].reshape(2 * PAGE, KDIM)
        m, l, o = weigh(q_rows[j], keys)
        last = meta_ref[END + j]
        has = meta_ref[END + j] > meta_ref[BEGIN + j]
        state = state_stats[last]
        m_state = jnp.where(has, state[:, 0:1], lowest)
        m_now = jnp.maximum(m, m_state)
        f = jnp.exp(m - m_now)
        g = jnp.where(has, jnp.exp(m_state - m_now), 0.0)
        l_now = l * f + state[:, 1:2] * g
        codes, scale = encode(o * f + states[last] * g)
        o_codes[:, j] = codes.reshape(RING_Y, rows // RING_Y, LAT)
        put_stats(c, j, m_now, l_now, scale)

        @pl.when(j == me)
        def _():
            s = jnp.where(new_visible, score(q_rows[j], new_keys), lowest)
            m_new = jnp.max(s, axis=1, keepdims=True)
            e = jnp.where(new_visible, jnp.exp(s - m_new), 0.0)
            l_new = jnp.sum(e, axis=1, keepdims=True)
            o_new = jnp.dot(
                e.astype(jnp.bfloat16), new_keys[:, :LAT], preferred_element_type=jnp.float32
            )
            m_all = jnp.maximum(m_now, m_new)
            old = jnp.exp(m_now - m_all)
            fresh_part = jnp.exp(m_new - m_all)
            mixed = (o * f + states[last] * g) * old + o_new * fresh_part
            codes, scale = encode(mixed)
            o_codes[:, j] = codes.reshape(RING_Y, rows // RING_Y, LAT)
            put_stats(c, j, m_all, l_now * old + l_new * fresh_part, scale)

    def put_stats(c, j, m, l, scale):
        block = stats[c].reshape(rows, 128)
        block = jnp.where(lane == 16 + j, l, jnp.where(lane == 32 + j, scale, block))
        stats[c] = jnp.where(lane == j, m, block).reshape(RING_Y, rows // RING_Y, 128)

    ways = (up, down)
    stat_far, stat_near, relayed, direct = {}, {}, {}, {}
    for c in range(CHUNKS):
        stats[c] = jnp.zeros((RING_Y, rows // RING_Y, 128), jnp.float32)

        def two_requests(i, _, c=c):
            whole_request(c, HALF * c + i)
            whole_request(c, 6 + HALF * c + i)
            return 0

        lax.fori_loop(0, HALF, two_requests, 0)
        for way, ahead in enumerate(ways):
            base = 6 * way + HALF * c
            first = 8 * c + 2 * way
            stat_far[c, way] = push(
                stats.at[c, far], stat_in.at[c, 2 * way], send_y, recv_y, first, at(z, ahead)
            )
            relayed[c, way] = push(
                o_codes.at[far, pl.ds(base, HALF)], relay_in.at[way, c], send_y, recv_y,
                first + 1, at(z, ahead),
            )
        for way, ahead in enumerate(ways):
            base = 6 * (1 - way) + HALF * c
            first = 8 * c + 4 + 2 * way
            stat_near[c, way] = push(
                stats.at[c, ahead], stat_in.at[c, 2 * way + 1], send_y, recv_y, first, at(z, ahead)
            )
            direct[c, way] = push(
                o_codes.at[ahead, pl.ds(base, HALF)], direct_in.at[way, c], send_y, recv_y,
                first + 1, at(z, ahead),
            )

    send_pages(BEFORE_ATTENTION, len(sent_pages))
    passed, passed_stat = {}, {}
    for c in range(CHUNKS):
        for way, ahead in enumerate(ways):
            stat_far[c, way].wait_recv()
            relayed[c, way].wait_recv()
            top, total, weights = merge_stats([stat_in[c, 2 * way], stats[c, ahead]])
            base = 6 * way + HALF * c

            def relay_one(i, scales, way=way, c=c, base=base, ahead=ahead, weights=weights):
                mixed = decode(relay_in[way, c, i]) * column(weights[0], base + i)
                mixed = mixed + decode(o_codes[ahead, base + i]) * column(weights[1], base + i)
                codes, scale = encode(mixed)
                merged[way, c, i] = codes
                at_lane = lax.broadcasted_iota(jnp.int32, scales.shape, 1)
                return jnp.where(at_lane == 32 + base + i, scale, scales)

            scales = lax.fori_loop(0, HALF, relay_one, jnp.zeros_like(top))
            mstat[way, c] = join_stats(top, total, scales)
            first = 8 * CHUNKS + 4 * c + 2 * way
            passed[c, way] = push(
                merged.at[way, c], merged_in.at[way, c], send_y, recv_y, first, at(z, ahead)
            )
            passed_stat[c, way] = push(
                mstat.at[way, c], mstat_in.at[way, c], send_y, recv_y, first + 1, at(z, ahead)
            )

    hand_over(0, 8)
    arrivals = {}
    for c in range(CHUNKS):
        merged_stats = []
        for way in range(2):
            stat_near[c, 1 - way].wait_recv()
            passed_stat[c, way].wait_recv()
            passed[c, way].wait_recv()
            direct[c, 1 - way].wait_recv()
            merged_stats.append(
                merge_stats([stats[c, y], mstat_in[way, c], stat_in[c, 2 * (1 - way) + 1]])
            )
        small = lax.broadcasted_iota(jnp.int32, (64, 128), 1)
        scales = jnp.zeros((64, 128), jnp.float32)
        for way in range(2):
            base = 6 * way + HALF * c
            weights = merged_stats[way][2]

            def land_one(i, scales, way=way, c=c, base=base, weights=weights):
                mixed = decode(o_codes[y, base + i]) * column(weights[0], base + i)
                mixed = mixed + decode(merged_in[way, c, i]) * column(weights[1], base + i)
                mixed = mixed + decode(direct_in[1 - way, c, i]) * column(weights[2], base + i)
                scale = jnp.maximum(jnp.max(jnp.abs(mixed), axis=1, keepdims=True), 1e-30)
                values[way * HALF + i] = jnp.floor(mixed * (CODE_TOP / scale) + 0.5)
                return jnp.where(small == 32 + base + i, scale * (1.0 / CODE_TOP), scales)

            scales = lax.fori_loop(0, HALF, land_one, scales)
        use_up = (small % 16) < 6
        top = jnp.where(use_up, merged_stats[0][0], merged_stats[1][0])
        total = jnp.where(use_up, merged_stats[0][1], merged_stats[1][1])
        zstat[c] = join_stats(top, total, scales)

        def split_one(zz, _, c=c):
            part = values[:, pl.ds(pl.multiple_of(zz * 8, 8), 8), :]
            part = part.reshape(2 * HALF * 8, LAT)
            zcodes[c, zz] = part.astype(jnp.int32).astype(jnp.int16)
            return 0

        lax.fori_loop(0, RING_Z, split_one, 0)
        for k in (4, 3, 5, 2, 6, 1, 7):
            there = (z + k) % RING_Z
            index = 2 * (c * RING_Z + k)
            arrivals[c, k] = (
                push(
                    zstat.at[c, pl.ds(there * 8, 8)], zstat_in.at[c, k], send_z, recv_z, index + 1,
                    at(there, y),
                ),
                push(zcodes.at[c, there], zin.at[c, k], send_z, recv_z, index, at(there, y)),
            )

    hand_over(8, len(sent_pages))
    for c in range(CHUNKS):
        for k in range(1, RING_Z):
            for copy in arrivals[c, k]:
                copy.wait_recv()
        finished = []
        blocks = [zstat[c, pl.ds(pl.multiple_of(z * 8, 8), 8), :]]
        blocks = blocks + [zstat_in[c, k] for k in range(1, RING_Z)]
        top, total, weights = merge_stats(blocks)
        for way in range(2):
            base = 6 * way + HALF * c
            sums = [1.0 / column(total, base + i) for i in range(HALF)]
            mixed = None
            for k in range(RING_Z):
                codes = zcodes.at[c, z] if k == 0 else zin.at[c, k]
                part = decode(codes[...])[way * HALF * 8 : (way + 1) * HALF * 8]
                factor = jnp.concatenate(
                    [column(weights[k], base + i) * sums[i] for i in range(HALF)], axis=0
                )
                mixed = part * factor if mixed is None else mixed + part * factor
            finished.append((base, mixed))
        for base, mixed in finished:
            out_f32[base * 8 : (base + HALF) * 8, :] = mixed
    out_ref[...] = out_f32[...].astype(jnp.bfloat16)
    keep_own.wait()
    for copy in over:
        copy.wait_recv()
    for copy in copies:
        copy.wait_send()


def decode_step(meta, queries, latents, own, gain, table, newtable):
    smem = pl.BlockSpec(memory_space=pltpu.SMEM)
    vmem = pl.BlockSpec(memory_space=pltpu.VMEM)
    hbm = pl.BlockSpec(memory_space=pl.ANY)
    pages = own.shape[0]
    rows = 8 * OWNERS
    half = (2, CHUNKS, HALF, 64, LAT)
    bf16, f32, i16 = jnp.bfloat16, jnp.float32, jnp.int16
    dma = pltpu.SemaphoreType.DMA
    return pl.pallas_call(
        decode_kernel,
        out_shape=(
            jax.ShapeDtypeStruct((96, LAT), bf16),
            jax.ShapeDtypeStruct((OWNERS, 2, PAGE, KDIM), bf16),
        ),
        in_specs=[smem, vmem, vmem, vmem, vmem, vmem, vmem],
        out_specs=(vmem, hbm),
        scratch_shapes=[
            pltpu.VMEM((4, 6, 16, KDIM), bf16),
            pltpu.VMEM((4, 3, 16, KDIM), bf16),
            pltpu.VMEM((OWNERS, 96, KDIM), bf16),
            pltpu.VMEM((12, rows, KDIM), bf16),
            pltpu.VMEM((pages, PAGE, KDIM), bf16),
            pltpu.VMEM((pages, PAGE, KDIM), bf16),
            pltpu.VMEM((OWNERS, PAGE, KDIM), bf16),
            pltpu.VMEM((pages + 1, rows, LAT), f32),
            pltpu.VMEM((pages + 1, rows, 2), f32),
            pltpu.VMEM((RING_Y, 12, rows // RING_Y, LAT), i16),
            pltpu.VMEM((CHUNKS, RING_Y, rows // RING_Y, 128), f32),
            pltpu.VMEM(half, i16),
            pltpu.VMEM(half, i16),
            pltpu.VMEM(half, i16),
            pltpu.VMEM(half, i16),
            pltpu.VMEM((CHUNKS, 4, 64, 128), f32),
            pltpu.VMEM((2, CHUNKS, 64, 128), f32),
            pltpu.VMEM((2, CHUNKS, 64, 128), f32),
            pltpu.VMEM((CHUNKS, RING_Z, 16 * HALF, LAT), i16),
            pltpu.VMEM((CHUNKS, RING_Z, 16 * HALF, LAT), i16),
            pltpu.VMEM((CHUNKS, 64, 128), f32),
            pltpu.VMEM((CHUNKS, RING_Z, 8, 128), f32),
            pltpu.VMEM((2 * HALF, 64, LAT), f32),
            pltpu.VMEM((96, LAT), f32),
            dma((8,)),
            dma((8,)),
            dma((64,)),
            dma((64,)),
            dma((OWNERS,)),
            dma((OWNERS,)),
            dma((OWNERS + 1,)),
            dma((OWNERS + 1,)),
            dma((12 * CHUNKS,)),
            dma((12 * CHUNKS,)),
            dma((2 * CHUNKS * RING_Z,)),
            dma((2 * CHUNKS * RING_Z,)),
            dma,
        ],
        compiler_params=pltpu.CompilerParams(
            vmem_limit_bytes=VMEM_LIMIT, collective_id=1, has_side_effects=True
        ),
        cost_estimate=pl.CostEstimate(
            flops=2_000_000_000, bytes_accessed=100_000_000, transcendentals=0
        ),
        name="decode_step",
    )(meta, queries, latents, own, gain.reshape(1, LAT), table, newtable)


def per_device(
    pool_pages,
    kv_gain,
    queries,
    decode_latent,
    served_request,
    resident_pages,
    resident_tail,
    page_dest,
):
    role = lax.axis_index("role")
    group = lax.axis_index("grp")
    owner = lax.axis_index("dev")
    own = pool_pages[0, 0, 0]
    pages_dev = own.shape[0]
    counts = resident_pages[0]
    tail_len = resident_tail[0]
    req_grp = counts.shape[0]
    steps = queries.shape[1]
    heads_here = queries.shape[2]
    per_prompt = pages_dev // req_grp
    span_len = per_prompt * PAGE * OWNERS
    res_len = PAGE * (counts - 1) + tail_len
    page_ids = jnp.arange(pages_dev, dtype=jnp.int32)
    positions = (
        res_len[:, None, None]
        + ((owner * per_prompt + jnp.arange(per_prompt, dtype=jnp.int32)) * PAGE)[None, :, None]
        + jnp.arange(PAGE, dtype=jnp.int32)[None, None, :]
    ).reshape(pages_dev, PAGE)
    mine = jnp.minimum(owner, req_grp - 1)
    my_len = jnp.sum(jnp.where(jnp.arange(req_grp) == mine, res_len, 0))
    new_positions = my_len + span_len + jnp.arange(16, dtype=jnp.int32) % steps

    targets = lax.dynamic_index_in_dim(page_dest[0], owner, 0, keepdims=False)
    wanted = jnp.arange(OWNERS, dtype=jnp.int32) * 2 + role
    hits = targets[None, :] == wanted[:, None]
    inverse = jnp.max(jnp.where(hits, page_ids[None, :], -1), axis=1)
    ids = jnp.arange(req_grp, dtype=jnp.int32)
    run_ends = jnp.sum(jnp.where(ids[None, :] <= ids[:, None], counts[None, :], 0), axis=1)
    starts = run_ends - counts
    flat = page_ids * OWNERS + owner
    begin = jnp.sum((flat[None, :] < starts[:, None]).astype(jnp.int32), axis=1)
    end = jnp.sum((flat[None, :] < run_ends[:, None]).astype(jnp.int32), axis=1)
    res_req = jnp.sum((flat[:, None] >= run_ends[None, :]).astype(jnp.int32), axis=1)
    whose = res_req[:, None] == ids[None, :]
    last_page = jnp.sum(jnp.where(whose, run_ends[None, :] - 1, 0), axis=1)
    last_tail = jnp.sum(jnp.where(whose, tail_len[None, :], 0), axis=1)
    valid = jnp.where(flat < last_page, PAGE, last_tail)
    first_of = jnp.sum(jnp.where(whose, begin[None, :], 0), axis=1)
    same = (page_ids > first_of).astype(jnp.int32)
    serving = lax.dynamic_slice_in_dim(served_request, group * req_grp, req_grp)
    meta = jnp.concatenate([serving, begin, end, res_req, valid, same, inverse]).astype(jnp.int32)

    attention, received = decode_step(
        meta, queries.reshape(6, 16, KDIM), decode_latent.reshape(3, 16, KDIM), own, kv_gain,
        rope_table(positions), rope_table(new_positions),
    )
    attention = attention.reshape(req_grp, steps, heads_here, LAT)
    received = received.reshape(1, 1, 2 * OWNERS, PAGE, KDIM)
    return (attention, received)


def solution(mesh):
    in_specs = (
        P("role", "grp", "dev", None, None, None),
        P(),
        P("grp", None, ("role", "dev"), None),
        P("grp", None, None),
        P(),
        P("grp", None),
        P("grp", None),
        P("grp", None, None),
    )
    out_specs = (P("grp", None, ("role", "dev"), None), P("grp", "dev", None, None, None))
    return jax.shard_map(
        per_device, mesh=mesh, in_specs=in_specs, out_specs=out_specs, check_vma=False
    )
```

time: 613 us -> 161 us (0.26)
  waiting for transfers between devices: 268 us -> 0 us
  other arithmetic: 151 us -> 7.87 us
  Pallas kernels: 0 us -> 138 us
  local copies, waits for them, and re-layouts: 68.8 us -> 12.5 us
  matrix products: 46 us -> 0 us
  starting transfers between devices: 36 us -> 0 us
  blocking collectives: 25.7 us -> 0 us
  between operations: 14.4 us -> 1.37 us
    all_to_all x4 -> x0, waiting for transfers between devices: 268 us -> none  [the longest x1 135 us: per_device(): lax.all_to_all(out_heads, 'dev', split_axis=2, concat_axis=0, tiled=True)]
    pallas_call x0 -> x1, Pallas kernels: none -> 138 us  [decode_step(): pl.pallas_call(decode_kernel, out_shape=(jax.ShapeDtypeStruct((96, LAT),...]
    scatter-add x8 -> x0, other arithmetic: 102 us -> none  [the longest x4 98.7 us: page_step(): (running_out * carry_over[..., None]).at[block_req]]
    dot_general x10 -> x0, matrix products: 46 us -> none  [the longest x4 23.4 us: page_step(): jnp.einsum('btq,btc->bqc', unnormed.astype(jnp.bfloat16), block_of_keys[....]
    gather x15 -> x0, local copies, waits for them, and re-layouts: 36 us -> none  [the longest x4 28.9 us: page_step(): local_queries = query_rows[block_req]]
    all_to_all x4 -> x0, starting transfers between devices: 35.4 us -> none  [the longest x1 11.8 us: per_device(): lax.all_to_all(outgoing, 'dev', split_axis=0, concat_axis=0, tiled=True)]
    all_gather x2 -> x0, blocking collectives: 25.7 us -> none  [the longest x1 13 us: per_device(): lax.all_gather(queries, 'grp', axis=0, tiled=True)]
    mul x8 -> x1, other arithmetic: 23.5 us -> 0.01 us  [per_device(): (owner * per_prompt + jnp.arange(per_prompt, dtype=jnp.int32)) * PAGE]
  transfers between devices with their start and end apart: 7 -> 0, of which waited for: 3 -> 0; matrix products, arithmetic and copies ran while one was open for 4% -> 0% of each run, Pallas kernels for 0% -> 0%
where the time goes in v2:
time: 161 us; the launch traced here: 159 us
  Pallas kernels  138 us (86%)
  local copies, waits for them, and re-layouts  12.5 us (8%)
  other arithmetic  7.87 us (5%)
    pallas_call x1, Pallas kernels, decode_step(): pl.pallas_call(decode_kernel, out_shape=(jax.ShapeDtypeStruct((96, LAT),...  138 us
    unnamed x3, local copies, waits for them, and re-layouts  5.97 us
    select_n x2, other arithmetic, rope_table(): return jnp.where(lane < 64, jnp.cos(angles), turned)  4.55 us

profile of v2, /device:TPU:16, one launch (start us, length us, event | category | flops | bytes accessed | tf_op | source)
XLA Modules:
  0.0 159.3 jit_solution(8968169963319644751)
XLA Ops:
  0.6 0.0 copy-start
  0.7 0.7 copy-done
  1.3 0.2 dynamic-slice_reduce_fusion
  1.5 0.1 select_reduce_fusion
  1.6 0.7 dynamic_slice.7
  2.4 0.8 select_reduce_fusion.4
  3.1 0.1 convert_reduce_fusion
  3.2 1.3 fusion.6
  5.2 0.2 convert_reduce_fusion.1
  5.4 0.7 select_reduce_fusion.1
  6.2 0.6 concatenate.3.meta_ref
  6.8 0.1 add.147
  6.9 0.1 add.148
  7.0 0.7 fusion.1.newtable_ref
  7.7 0.1 add.152
  7.8 0.1 add_convert_fusion
  7.9 1.5 reshape.159.lat_ref
  9.4 1.6 %reshape.158.q_ref = bf16[6,16,576]{2,1,0:T(8,128)(2,1)} reshape(bf16[12,4,2,576]{3,2,1,0:T(2,128)(2,1)} %param.10) | data formatting | bytes 221184 | tf_op jit(solution)/shard_map/reshape | solution.py:666
  11.0 3.8 %fusion.table_ref = f32[24,64,128]{2,1,0:T(8,128)} fusion(f32[128]{0:T(128)S(1)} %fusion.5, f32[24,64]{1,0:T(8,128)S(1)} %add_convert_fusion, pred[128]{0:T(512)(128)(4,1)S(1)} %get-tuple-element.15, pred[128]{0:T(512)(128)(4,1)S(1)} %get-tuple-element.16), kind=kLoop, calls=%fused_computation.3 | loop fusion | flops 786432 | bytes 793344 | tf_op jit(solution)/shard_map/jit(_where)/select_n | solution.py:32
  14.8 137.6 %decode_step.1 = (bf16[96,512]{1,0:T(8,128)(2,1)}, bf16[32,2,64,576]{3,2,1,0:T(8,128)(2,1)}) custom-call(s32[140]{0:T(256)} %concatenate.3.meta_ref, bf16[6,16,576]{2,1,0:T(8,128)(2,1)} %reshape.158.q_ref, bf16[3,16,576]{2,1,0:T(8,128)(2,1)} %reshape.159.lat_ref, bf16[24,64,576]{2,1,0:T(8,128)(2,1)} %bitcast.15, f32[1,512]{1,0:T(1,128)} %bitcast.16, ...), custom_call_target="tpu_custom_call" | custom-call | flops 2000000000 | bytes 100000000 | tf_op jit(solution)/shard_map/decode_step/pallas_call | solution.py:555
  152.4 1.6 reshape.161
  154.0 5.3 %copy.11 = bf16[1,1,64,64,576]{4,3,2,1,0:T(8,128)(2,1)} copy(bf16[1,1,64,64,576]{4,3,2,1,0:T(8,128)(2,1)} %bitcast.12) | data formatting | bytes 9437184
  (10 shorter events, 0.1 us)
Async XLA Ops:
  0.6 0.7 copy-start

commit v3 on v2

--- a/solution.py
+++ b/solution.py
@@ -20,13 +20,12 @@
 RING_Z = 8
 
 
-SERVED, BEGIN, END, REQUEST, VALID, SAME, INVERSE = 0, 12, 24, 36, 60, 84, 108
-
-
-def rope_table(positions):
-    lane = jnp.arange(128)
-    frequency = 10000.0 ** (-(lane % 32).astype(jnp.float32) / 32)
-    angles = positions[..., None].astype(jnp.float32) * frequency
+BEGIN, END, RUN_END, REQUEST, VALID, SAME, INVERSE = 0, 12, 24, 36, 60, 84, 108
+
+
+def rope_table(positions, frequency):
+    lane = lax.broadcasted_iota(jnp.int32, positions.shape, 1)
+    angles = positions.astype(jnp.float32) * frequency
     sine_part = jnp.sin(angles)
     turned = jnp.where(lane < 96, -sine_part, sine_part)
     return jnp.where(lane < 64, jnp.cos(angles), turned)
@@ -34,14 +33,14 @@
 
 MESH_IDS = pl.DeviceIdType.MESH
 CODE_TOP = 32767.0
-CHUNKS = 2
+CHUNKS = 3
 HALF = 6 // CHUNKS
 
 
 DISTANCES = [(0, dy) for dy in (2, 1, 3)]
 DISTANCES = DISTANCES + [(dz, dy) for dy in (1, 3, 2, 0) for dz in (4, 3, 5, 2, 6, 1, 7)]
 DISTANCES = DISTANCES + [(0, 0)]
-EARLY, BEFORE_ATTENTION = 6, 20
+EARLY, BEFORE_ATTENTION = 0, 20
 
 
 def everyone(role, group, z, y):
@@ -92,10 +91,11 @@
 
 
 def decode_kernel(
-    meta_ref, q_ref, lat_ref, own_ref, gain_ref, table_ref, newtable_ref,
+    served_ref, counts_ref, tail_ref, dest_ref, q_ref, lat_ref, own_ref, gain_ref, frequency_ref,
     out_ref, cache_ref,
+    meta_ref, table,
     xbuf, lbuf, q_all, q_rows, partner, fresh, outgoing,
-    states, state_stats, o_codes, stats,
+    states, state_m, state_l, o_codes, stats,
     relay_in, direct_in, merged, merged_in, stat_in, mstat, mstat_in,
     zcodes, zin, zstat, zstat_in, values, out_f32,
     send_x, recv_x, send_q, recv_q, send_page, recv_page, send_role, recv_role,
@@ -146,11 +146,55 @@
         arriving_latents.append(push(lat_ref, lbuf.at[group], send_x, recv_x, 2 * k + 1, target))
     xbuf[group] = q_ref[...]
     lbuf[group] = lat_ref[...]
+
+    def served(j):
+        return served_ref[group * 12 + j]
+
+    def context(j):
+        return PAGE * (counts_ref[0, j] - 1) + tail_ref[0, j]
+
+    run = 0
+    for j in range(12):
+        meta_ref[BEGIN + j] = (run - me + OWNERS - 1) // OWNERS
+        run = run + counts_ref[0, j]
+        meta_ref[END + j] = (run - me + OWNERS - 1) // OWNERS
+        meta_ref[RUN_END + j] = run
+
+    def describe(x, _):
+        flat = x * OWNERS + me
+        request = 0
+        for j in range(11):
+            request = request + (flat >= meta_ref[RUN_END + j]).astype(jnp.int32)
+        meta_ref[REQUEST + x] = request
+        meta_ref[VALID + x] = jnp.where(
+            flat < meta_ref[RUN_END + request] - 1, PAGE, tail_ref[0, request]
+        )
+        meta_ref[SAME + x] = (x > meta_ref[BEGIN + request]).astype(jnp.int32)
+        return 0
+
+    lax.fori_loop(0, pages, describe, 0)
+
+    def invert(t, _):
+        page = -1
+        for i in range(24):
+            page = jnp.where(dest_ref[me, i] == 2 * t + role, i, page)
+        meta_ref[INVERSE + t] = page
+        return 0
+
+    lax.fori_loop(0, OWNERS, invert, 0)
+    frequency = frequency_ref[...]
+    token = lax.broadcasted_iota(jnp.int32, (PAGE, 128), 0)
+
+    def one_table(i, _):
+        base = context(i // 2) + (me * 2 + i % 2) * PAGE
+        table[i] = rope_table(base + token, frequency)
+        return 0
+
+    lax.fori_loop(0, pages, one_table, 0)
+    new_base = context(jnp.minimum(me, 11)) + 2 * OWNERS * PAGE
+    new_table = rope_table(new_base + token[:16] % 4, frequency)
     for copy in arriving:
         copy.wait_recv()
-
-    def served(j):
-        return meta_ref[SERVED + j]
 
     def pick(index):
         pair = xbuf[index // 12, (index % 12) // 2].astype(jnp.float32)
@@ -218,18 +262,18 @@
     exchange.wait_recv()
     gain = gain_ref[...]
 
-    def finish(raw, table):
+    def finish(raw, turns):
         latent = raw[:, :LAT]
         mean_square = jnp.sum(latent * latent, axis=-1, keepdims=True) * (1.0 / LAT)
         normed = latent * lax.rsqrt(mean_square + epsilon) * gain
         rope = raw[:, LAT:]
         swapped = jnp.concatenate([rope[:, 32:], rope[:, :32]], axis=-1)
-        turned = rope * table[:, :64] + swapped * table[:, 64:]
+        turned = rope * turns[:, :64] + swapped * turns[:, 64:]
         return jnp.concatenate([normed, turned], axis=-1).astype(jnp.bfloat16)
 
     def one_page(i, _):
         raw = jnp.where(at_prefill, own_ref[i], partner[i]).astype(jnp.float32)
-        fresh[i] = finish(raw, table_ref[i])
+        fresh[i] = finish(raw, table[i])
         return 0
 
     third = pages // 3
@@ -301,7 +345,8 @@
         return s * logit_scale_factor
 
     states[0] = jnp.zeros((rows, LAT), jnp.float32)
-    state_stats[0] = jnp.zeros((rows, 2), jnp.float32)
+    state_m[0] = jnp.zeros((rows, 128), jnp.float32)
+    state_l[0] = jnp.zeros((rows, 128), jnp.float32)
     page_lane = lax.broadcasted_iota(jnp.int32, (rows, PAGE), 1)
 
     def page_terms(x):
@@ -315,17 +360,26 @@
         o = jnp.dot(e.astype(jnp.bfloat16), keys[:, :LAT], preferred_element_type=jnp.float32)
         return m, l, o
 
+    def wide(column_values):
+        return jnp.broadcast_to(column_values, (rows, 128))
+
+    def blend(left, a, right, b):
+        tiles = [
+            left[:, k : k + 128] * a + right[:, k : k + 128] * b for k in range(0, LAT, 128)
+        ]
+        return jnp.concatenate(tiles, axis=1)
+
     def chain(x, terms):
         m, l, o = terms
         same = meta_ref[SAME + x] == 1
-        before = state_stats[x]
-        m_before = jnp.where(same, before[:, 0:1], lowest)
+        m = wide(m)
+        m_before = jnp.where(same, state_m[x], lowest)
         m_now = jnp.maximum(m, m_before)
         carry = jnp.where(same, jnp.exp(m_before - m_now), 0.0)
         f = jnp.exp(m - m_now)
-        l_now = before[:, 1:2] * carry + l * f
-        state_stats[x + 1] = jnp.concatenate([m_now, l_now], axis=1)
-        states[x + 1] = states[x] * carry + o * f
+        state_m[x + 1] = m_now
+        state_l[x + 1] = state_l[x] * carry + wide(l) * f
+        states[x + 1] = blend(states[x], carry, o, f)
 
     def two_resident(i, _):
         terms = [page_terms(2 * i), page_terms(2 * i + 1)]
@@ -340,7 +394,7 @@
 
     mine = served(jnp.minimum(me, 11))
     new_raw = lbuf[mine // 12, (mine % 12) // 4].astype(jnp.float32)
-    new_keys = finish(new_raw, newtable_ref[...])
+    new_keys = finish(new_raw, new_table)
     new_keys = jnp.concatenate(
         [new_keys, jnp.zeros((2 * PAGE - 16, KDIM), jnp.bfloat16)], axis=0
     )
@@ -371,13 +425,13 @@
         m, l, o = weigh(q_rows[j], keys)
         last = meta_ref[END + j]
         has = meta_ref[END + j] > meta_ref[BEGIN + j]
-        state = state_stats[last]
-        m_state = jnp.where(has, state[:, 0:1], lowest)
+        m = wide(m)
+        m_state = jnp.where(has, state_m[last], lowest)
         m_now = jnp.maximum(m, m_state)
         f = jnp.exp(m - m_now)
         g = jnp.where(has, jnp.exp(m_state - m_now), 0.0)
-        l_now = l * f + state[:, 1:2] * g
-        codes, scale = encode(o * f + states[last] * g)
+        l_now = wide(l) * f + state_l[last] * g
+        codes, scale = encode(blend(o, f, states[last], g))
         o_codes[:, j] = codes.reshape(RING_Y, rows // RING_Y, LAT)
         put_stats(c, j, m_now, l_now, scale)
 
@@ -390,13 +444,14 @@
             o_new = jnp.dot(
                 e.astype(jnp.bfloat16), new_keys[:, :LAT], preferred_element_type=jnp.float32
             )
+            m_new = wide(m_new)
             m_all = jnp.maximum(m_now, m_new)
             old = jnp.exp(m_now - m_all)
             fresh_part = jnp.exp(m_new - m_all)
-            mixed = (o * f + states[last] * g) * old + o_new * fresh_part
+            mixed = blend(blend(o, f, states[last], g), old, o_new, fresh_part)
             codes, scale = encode(mixed)
             o_codes[:, j] = codes.reshape(RING_Y, rows // RING_Y, LAT)
-            put_stats(c, j, m_all, l_now * old + l_new * fresh_part, scale)
+            put_stats(c, j, m_all, l_now * old + wide(l_new) * fresh_part, scale)
 
     def put_stats(c, j, m, l, scale):
         block = stats[c].reshape(rows, 128)
@@ -405,7 +460,7 @@
 
     ways = (up, down)
     stat_far, stat_near, relayed, direct = {}, {}, {}, {}
-    for c in range(CHUNKS):
+    def attend(c):
         stats[c] = jnp.zeros((RING_Y, rows // RING_Y, 128), jnp.float32)
 
         def two_requests(i, _, c=c):
@@ -435,9 +490,8 @@
                 first + 1, at(z, ahead),
             )
 
-    send_pages(BEFORE_ATTENTION, len(sent_pages))
     passed, passed_stat = {}, {}
-    for c in range(CHUNKS):
+    def relay(c):
         for way, ahead in enumerate(ways):
             stat_far[c, way].wait_recv()
             relayed[c, way].wait_recv()
@@ -462,9 +516,9 @@
                 mstat.at[way, c], mstat_in.at[way, c], send_y, recv_y, first + 1, at(z, ahead)
             )
 
-    hand_over(0, 8)
     arrivals = {}
-    for c in range(CHUNKS):
+
+    def land(c):
         merged_stats = []
         for way in range(2):
             stat_near[c, 1 - way].wait_recv()
@@ -512,6 +566,15 @@
                 push(zcodes.at[c, there], zin.at[c, k], send_z, recv_z, index, at(there, y)),
             )
 
+    for c in range(CHUNKS):
+        attend(c)
+        if c >= 1:
+            relay(c - 1)
+    send_pages(BEFORE_ATTENTION, len(sent_pages))
+    relay(CHUNKS - 1)
+    hand_over(0, 8)
+    for c in range(CHUNKS):
+        land(c)
     hand_over(8, len(sent_pages))
     for c in range(CHUNKS):
         for k in range(1, RING_Z):
@@ -543,7 +606,7 @@
         copy.wait_send()
 
 
-def decode_step(meta, queries, latents, own, gain, table, newtable):
+def decode_step(served, counts, tails, dest, queries, latents, own, gain, frequency):
     smem = pl.BlockSpec(memory_space=pltpu.SMEM)
     vmem = pl.BlockSpec(memory_space=pltpu.VMEM)
     hbm = pl.BlockSpec(memory_space=pl.ANY)
@@ -558,9 +621,11 @@
             jax.ShapeDtypeStruct((96, LAT), bf16),
             jax.ShapeDtypeStruct((OWNERS, 2, PAGE, KDIM), bf16),
         ),
-        in_specs=[smem, vmem, vmem, vmem, vmem, vmem, vmem],
+        in_specs=[smem, smem, smem, smem, vmem, vmem, vmem, vmem, vmem],
         out_specs=(vmem, hbm),
         scratch_shapes=[
+            pltpu.SMEM((144,), jnp.int32),
+            pltpu.VMEM((pages, PAGE, 128), f32),
             pltpu.VMEM((4, 6, 16, KDIM), bf16),
             pltpu.VMEM((4, 3, 16, KDIM), bf16),
             pltpu.VMEM((OWNERS, 96, KDIM), bf16),
@@ -569,7 +634,8 @@
             pltpu.VMEM((pages, PAGE, KDIM), bf16),
             pltpu.VMEM((OWNERS, PAGE, KDIM), bf16),
             pltpu.VMEM((pages + 1, rows, LAT), f32),
-            pltpu.VMEM((pages + 1, rows, 2), f32),
+            pltpu.VMEM((pages + 1, rows, 128), f32),
+            pltpu.VMEM((pages + 1, rows, 128), f32),
             pltpu.VMEM((RING_Y, 12, rows // RING_Y, LAT), i16),
             pltpu.VMEM((CHUNKS, RING_Y, rows // RING_Y, 128), f32),
             pltpu.VMEM(half, i16),
@@ -606,7 +672,7 @@
             flops=2_000_000_000, bytes_accessed=100_000_000, transcendentals=0
         ),
         name="decode_step",
-    )(meta, queries, latents, own, gain.reshape(1, LAT), table, newtable)
+    )(served, counts, tails, dest, queries, latents, own, gain.reshape(1, LAT), frequency)
 
 
 def per_device(
@@ -619,52 +685,15 @@
     resident_tail,
     page_dest,
 ):
-    role = lax.axis_index("role")
-    group = lax.axis_index("grp")
-    owner = lax.axis_index("dev")
     own = pool_pages[0, 0, 0]
-    pages_dev = own.shape[0]
-    counts = resident_pages[0]
-    tail_len = resident_tail[0]
-    req_grp = counts.shape[0]
+    req_grp = resident_pages.shape[1]
     steps = queries.shape[1]
     heads_here = queries.shape[2]
-    per_prompt = pages_dev // req_grp
-    span_len = per_prompt * PAGE * OWNERS
-    res_len = PAGE * (counts - 1) + tail_len
-    page_ids = jnp.arange(pages_dev, dtype=jnp.int32)
-    positions = (
-        res_len[:, None, None]
-        + ((owner * per_prompt + jnp.arange(per_prompt, dtype=jnp.int32)) * PAGE)[None, :, None]
-        + jnp.arange(PAGE, dtype=jnp.int32)[None, None, :]
-    ).reshape(pages_dev, PAGE)
-    mine = jnp.minimum(owner, req_grp - 1)
-    my_len = jnp.sum(jnp.where(jnp.arange(req_grp) == mine, res_len, 0))
-    new_positions = my_len + span_len + jnp.arange(16, dtype=jnp.int32) % steps
-
-    targets = lax.dynamic_index_in_dim(page_dest[0], owner, 0, keepdims=False)
-    wanted = jnp.arange(OWNERS, dtype=jnp.int32) * 2 + role
-    hits = targets[None, :] == wanted[:, None]
-    inverse = jnp.max(jnp.where(hits, page_ids[None, :], -1), axis=1)
-    ids = jnp.arange(req_grp, dtype=jnp.int32)
-    run_ends = jnp.sum(jnp.where(ids[None, :] <= ids[:, None], counts[None, :], 0), axis=1)
-    starts = run_ends - counts
-    flat = page_ids * OWNERS + owner
-    begin = jnp.sum((flat[None, :] < starts[:, None]).astype(jnp.int32), axis=1)
-    end = jnp.sum((flat[None, :] < run_ends[:, None]).astype(jnp.int32), axis=1)
-    res_req = jnp.sum((flat[:, None] >= run_ends[None, :]).astype(jnp.int32), axis=1)
-    whose = res_req[:, None] == ids[None, :]
-    last_page = jnp.sum(jnp.where(whose, run_ends[None, :] - 1, 0), axis=1)
-    last_tail = jnp.sum(jnp.where(whose, tail_len[None, :], 0), axis=1)
-    valid = jnp.where(flat < last_page, PAGE, last_tail)
-    first_of = jnp.sum(jnp.where(whose, begin[None, :], 0), axis=1)
-    same = (page_ids > first_of).astype(jnp.int32)
-    serving = lax.dynamic_slice_in_dim(served_request, group * req_grp, req_grp)
-    meta = jnp.concatenate([serving, begin, end, res_req, valid, same, inverse]).astype(jnp.int32)
-
+    frequency = 10000.0 ** (-(jnp.arange(128) % 32).astype(jnp.float32) / 32)
     attention, received = decode_step(
-        meta, queries.reshape(6, 16, KDIM), decode_latent.reshape(3, 16, KDIM), own, kv_gain,
-        rope_table(positions), rope_table(new_positions),
+        served_request, resident_pages, resident_tail, page_dest[0],
+        queries.reshape(6, 16, KDIM), decode_latent.reshape(3, 16, KDIM), own, kv_gain,
+        frequency.reshape(1, 128),
     )
     attention = attention.reshape(req_grp, steps, heads_here, LAT)
     received = received.reshape(1, 1, 2 * OWNERS, PAGE, KDIM)

time: 161 us -> 145 us (0.901)
  other arithmetic: 7.87 us -> 0.53 us
  Pallas kernels: 138 us -> 132 us
    pallas_call x1, Pallas kernels: 138 us -> 132 us  [decode_step(): pl.pallas_call(decode_kernel, out_shape=(jax.ShapeDtypeStruct((96, LAT),...]
    select_n x3 -> x0, other arithmetic: 4.56 us -> none  [the longest x2 4.55 us: rope_table(): return jnp.where(lane < 64, jnp.cos(angles), turned)]
    reduce_sum x5 -> x0, other arithmetic: 3.11 us -> none  [the longest x1 1.31 us: per_device(): my_len = jnp.sum(jnp.where(jnp.arange(req_grp) == mine, res_len, 0))]
    unnamed x3 -> x2, local copies, waits for them, and re-layouts: 5.97 us -> 6.68 us
where the time goes in v3:
time: 145 us
  Pallas kernels  132 us (91%)
  local copies, waits for them, and re-layouts  11.4 us (8%)
    pallas_call x1, Pallas kernels, decode_step(): pl.pallas_call(decode_kernel, out_shape=(jax.ShapeDtypeStruct((96, LAT),...  132 us
    unnamed x2, local copies, waits for them, and re-layouts  6.68 us

profile of v3, /device:TPU:16, one launch (start us, length us, event | category | flops | bytes accessed | tf_op | source)
XLA Modules:
  0.0 144.9 jit_solution(9033372470268265953)
XLA Ops:
  0.6 0.5 fusion.3.frequency_ref
  1.2 1.4 copy.10
  2.5 1.5 %reshape.55.lat_ref = bf16[3,16,576]{2,1,0:T(8,128)(2,1)} reshape(bf16[12,4,576]{2,1,0:T(4,128)(2,1)} %param.11) | data formatting | bytes 110592 | tf_op jit(solution)/shard_map/reshape | solution.py:695
  4.0 1.6 %reshape.54.q_ref = bf16[6,16,576]{2,1,0:T(8,128)(2,1)} reshape(bf16[12,4,2,576]{3,2,1,0:T(2,128)(2,1)} %param.10) | data formatting | bytes 221184 | tf_op jit(solution)/shard_map/reshape | solution.py:695
  5.7 132.4 %decode_step.1 = (bf16[96,512]{1,0:T(8,128)(2,1)}, bf16[32,2,64,576]{3,2,1,0:T(8,128)(2,1)}) custom-call(s32[48]{0:T(128)} %served_ref.1, s32[1,12]{1,0:T(1,128)} %counts_ref.1, s32[1,12]{1,0:T(1,128)} %tail_ref.1, s32[32,24]{1,0:T(8,128)} %bitcast.5, bf16[6,16,576]{2,1,0:T(8,128)(2,1)} %reshape.54.q_ref, bf16[3,16,576]{2,1,0:T(8,128)(2,1)} %reshape.55.lat_ref, ...), custom_call_target="tpu_custom_call" | custom-call | flops 2000000000 | bytes 100000000 | tf_op jit(solution)/shard_map/decode_step/pallas_call | solution.py:618
  138.0 1.6 %reshape.57 = bf16[12,4,2,512]{3,2,1,0:T(2,128)(2,1)} reshape(bf16[96,512]{1,0:T(8,128)(2,1)} %get-tuple-element.4) | data formatting | bytes 196608 | tf_op jit(solution)/shard_map/reshape | solution.py:698
  139.6 5.3 %copy.12 = bf16[1,1,64,64,576]{4,3,2,1,0:T(8,128)(2,1)} copy(bf16[1,1,64,64,576]{4,3,2,1,0:T(8,128)(2,1)} %bitcast.4) | data formatting | bytes 9437184

commit v4 on v3

--- a/solution.py
+++ b/solution.py
@@ -38,9 +38,10 @@
 
 
 DISTANCES = [(0, dy) for dy in (2, 1, 3)]
-DISTANCES = DISTANCES + [(dz, dy) for dy in (1, 3, 2, 0) for dz in (4, 3, 5, 2, 6, 1, 7)]
+DISTANCES = DISTANCES + [(dz, dy) for dz in (4, 3, 5, 2, 6, 1, 7) for dy in (2, 1, 3)]
+DISTANCES = DISTANCES + [(dz, 0) for dz in (4, 3, 5, 2, 6, 1, 7)]
 DISTANCES = DISTANCES + [(0, 0)]
-EARLY, BEFORE_ATTENTION = 0, 20
+EARLY, BEFORE_ATTENTION = 0, 31
 
 
 def everyone(role, group, z, y):

time: 145 us -> 143 us (0.986)
  Pallas kernels: 132 us -> 129 us
    pallas_call x1, Pallas kernels: 132 us -> 129 us  [decode_step(): pl.pallas_call(decode_kernel, out_shape=(jax.ShapeDtypeStruct((96, LAT),...]
where the time goes in v4:
time: 143 us; the launch traced here: 142 us
  Pallas kernels  129 us (90%)
  local copies, waits for them, and re-layouts  11.4 us (8%)
    pallas_call x1, Pallas kernels, decode_step(): pl.pallas_call(decode_kernel, out_shape=(jax.ShapeDtypeStruct((96, LAT),...  129 us
    unnamed x2, local copies, waits for them, and re-layouts  6.68 us

profile of v4, /device:TPU:16, one launch (start us, length us, event | category | flops | bytes accessed | tf_op | source)
XLA Modules:
  0.0 141.6 jit_solution(3829216091666425384)
XLA Ops:
  0.6 0.5 fusion.3.frequency_ref
  1.2 1.4 copy.10
  2.5 1.5 %reshape.55.lat_ref = bf16[3,16,576]{2,1,0:T(8,128)(2,1)} reshape(bf16[12,4,576]{2,1,0:T(4,128)(2,1)} %param.11) | data formatting | bytes 110592 | tf_op jit(solution)/shard_map/reshape | solution.py:696
  4.0 1.6 %reshape.54.q_ref = bf16[6,16,576]{2,1,0:T(8,128)(2,1)} reshape(bf16[12,4,2,576]{3,2,1,0:T(2,128)(2,1)} %param.10) | data formatting | bytes 221184 | tf_op jit(solution)/shard_map/reshape | solution.py:696
  5.7 129.0 %decode_step.1 = (bf16[96,512]{1,0:T(8,128)(2,1)}, bf16[32,2,64,576]{3,2,1,0:T(8,128)(2,1)}) custom-call(s32[48]{0:T(128)} %served_ref.1, s32[1,12]{1,0:T(1,128)} %counts_ref.1, s32[1,12]{1,0:T(1,128)} %tail_ref.1, s32[32,24]{1,0:T(8,128)} %bitcast.5, bf16[6,16,576]{2,1,0:T(8,128)(2,1)} %reshape.54.q_ref, bf16[3,16,576]{2,1,0:T(8,128)(2,1)} %reshape.55.lat_ref, ...), custom_call_target="tpu_custom_call" | custom-call | flops 2000000000 | bytes 100000000 | tf_op jit(solution)/shard_map/decode_step/pallas_call | solution.py:619
  134.7 1.6 %reshape.57 = bf16[12,4,2,512]{3,2,1,0:T(2,128)(2,1)} reshape(bf16[96,512]{1,0:T(8,128)(2,1)} %get-tuple-element.4) | data formatting | bytes 196608 | tf_op jit(solution)/shard_map/reshape | solution.py:699
  136.3 5.3 %copy.12 = bf16[1,1,64,64,576]{4,3,2,1,0:T(8,128)(2,1)} copy(bf16[1,1,64,64,576]{4,3,2,1,0:T(8,128)(2,1)} %bitcast.4) | data formatting | bytes 9437184
